TPU v7x, 512 devices: a whole 4x8x8 slice. The times are simulated.
512 devices in a mesh: kx: 64 (over z, x, core), gy: 8 (over y).
Axes of the slice: x: 4, y: 8, z: 8, core: 2. Of those that a mesh axis runs over, the one named last changes fastest.
Arguments:
- line_values: float32 [73728, 768], P(('kx', 'gy')), may hold values from -6 to 6
- line_ids: int32 [73728], P(('kx', 'gy')), may hold values from -1 to 147455, as said below
- line_start: int32 [73728], P(('kx', 'gy')), may hold values from 0 to 5, as said below
- line_stop: int32 [73728], P(('kx', 'gy')), may hold values from 1 to 6
- spectrum_real: float32 [64, 768, 768], P('kx', 'gy'), may hold values from -6 to 6
- spectrum_imag: float32 [64, 768, 768], P('kx', 'gy'), may hold values from -6 to 6
Outputs:
- product_real: float32 [64, 768, 768], P('kx', 'gy')
- product_imag: float32 [64, 768, 768], P('kx', 'gy')
Inputs may be any that keep to these rules, and one draw needn't show every extreme that they name: `line_ids`: slot s belongs to device block s // 144, which is k * (number of gy devices) + g for the device at index k of kx and g of gy; a used slot there holds a line y * 384 + z with y in [g * 48, (g + 1) * 48) and z in [k * 6, (k + 1) * 6). No line is held twice. Each device block has at most 144 used slots, and some block has exactly 144. Every slot has line_start < line_stop.
All inputs are finite; a program needn't handle non-finite values.
Results may differ from a plain program's by a relative error of at most 0.0003.
Values sent between devices are 32-bit elements; how exact they have to be, the bound alone decides.
No kernel may reach another device: no remote copies, remote signals or barrier semaphores. Data moves between devices by JAX's collectives and lax.ppermute only.
A program may use at most 64 MiB of HBM per device.

v0:
```python
import math

import jax
import jax.numpy as jnp
from jax import lax
from jax.sharding import PartitionSpec as P

NG = 384
BLK = 64


HIGHEST = lax.Precision.HIGHEST


def angle_tables(inputs_count, outputs_count, length):
    rows_index = jnp.arange(inputs_count, dtype=jnp.int32)[:, None]
    wave_index = jnp.arange(outputs_count, dtype=jnp.int32)[None, :]
    phase_index = rows_index * wave_index % length
    angles = phase_index.astype(jnp.float32) * (2.0 * math.pi / length)
    return (jnp.cos(angles), jnp.sin(angles))


def complex_table(inputs_count, outputs_count, length):
    cosine, sine_part = angle_tables(inputs_count, outputs_count, length)
    first_rows = jnp.concatenate([cosine, -sine_part], axis=1)
    second_rows = jnp.concatenate([sine_part, cosine], axis=1)
    return jnp.concatenate([first_rows, second_rows], axis=0)


def occupied_values(line_values, line_start, line_stop):
    position = jnp.arange(NG, dtype=jnp.int32)[None, :]
    inside = (position >= BLK * line_start[:, None]) & (position < BLK * line_stop[:, None])
    weight = inside.astype(jnp.float32)
    return line_values * jnp.concatenate([weight, weight], axis=1)


def on_device(line_values, line_ids, line_start, line_stop, spectrum_real, spectrum_imag):
    kx_count = lax.axis_size("kx")
    gy_count = lax.axis_size("gy")
    plane_count = spectrum_real.shape[0]
    window = plane_count * kx_count
    row_count = NG // gy_count
    depth_count = NG // kx_count
    kx_here = lax.axis_index("kx")
    gy_here = lax.axis_index("gy")
    values = occupied_values(line_values, line_start, line_stop)
    x_table = complex_table(NG, window, 2 * NG).reshape(2 * NG, 2, window)
    wave_table = complex_table(NG, 2 * NG, 2 * NG)
    split_table = wave_table.reshape(2, NG, 4 * NG)
    row_local = line_ids // NG - gy_here * row_count
    col_local = line_ids % NG - kx_here * depth_count
    target = jnp.where(line_ids >= 0, row_local * depth_count + col_local, row_count * depth_count)
    dense_grid = (
        jnp.zeros((row_count * depth_count, 2 * NG), jnp.float32)
        .at[target]
        .add(values, mode="drop")
    )
    dense_grid = dense_grid.reshape(row_count, depth_count, 2 * NG)
    x_spectrum = jnp.einsum("yzn,nck->kycz", dense_grid, x_table, precision=HIGHEST)
    x_spectrum = x_spectrum.reshape(window, 1, row_count * 2 * depth_count)
    arrived = lax.all_to_all(x_spectrum, "kx", split_axis=0, concat_axis=2, tiled=True)
    item_count = arrived.shape[1]
    source_count = arrived.shape[2] // (row_count * 2 * depth_count)
    blocks = arrived.reshape(plane_count, item_count, source_count, row_count, 2, depth_count)
    blocks = jnp.transpose(blocks, (0, 1, 3, 4, 2, 5))
    flat_rows = blocks.reshape(plane_count * item_count * row_count, 2 * NG)
    result = jnp.dot(flat_rows, wave_table, precision=HIGHEST)
    z_spectrum = result.reshape(plane_count, item_count, row_count, 2, 2 * NG)
    z_spectrum = z_spectrum.reshape(plane_count, row_count, 2, 2 * NG)
    pencils = lax.all_to_all(z_spectrum, "gy", split_axis=3, concat_axis=1, tiled=True)
    item_count = pencils.shape[0]
    wave_rows = pencils.shape[3]
    result = jnp.einsum("aycq,cyd->aqd", pencils, split_table, precision=HIGHEST)
    full_spectrum = result.reshape(item_count, wave_rows, 2, 2 * NG)
    real_part = full_spectrum[:, :, 0, :]
    imag_part = full_spectrum[:, :, 1, :]
    scale_factor = float(NG) ** (-1.5)
    product_real = scale_factor * (spectrum_real * real_part - spectrum_imag * imag_part)
    product_imag = scale_factor * (spectrum_real * imag_part + spectrum_imag * real_part)
    return (product_real, product_imag)


def solution(mesh):
    in_specs = (
        P(("kx", "gy"), None),
        P(("kx", "gy")),
        P(("kx", "gy")),
        P(("kx", "gy")),
        P("kx", "gy", None),
        P("kx", "gy", None),
    )
    out_specs = (P("kx", "gy", None), P("kx", "gy", None))
    return jax.shard_map(
        on_device, mesh=mesh, in_specs=in_specs, out_specs=out_specs, check_vma=False
    )
```

profile of v0, /device:TPU:1, one launch (start us, length us, event | category | flops | bytes accessed | tf_op | source)
XLA Modules:
  0.0 83.0 jit_solution(8942206206723070794)
XLA Ops:
  0.6 0.4 fusion.24
  1.0 0.4 fusion.27
  1.5 0.7 broadcast_multiply_fusion
  2.2 0.1 fusion.19
  2.3 0.7 compare_select_fusion
  3.0 2.2 %scatter_custom_fusion = f32[288,768]{1,0:T(8,128)S(1)} fusion(s32[144]{0:T(256)S(1)} %compare_select_fusion, f32[144,768]{1,0:T(8,128)} %param.6, f32[]{:T(128)} %constant.34.clone.1, pred[144,384]{1,0:T(8,128)(4,1)S(1)} %fusion.19, pred[]{:T(512)} %constant.72), kind=kCustom, calls=%fused_computation.17 | custom fusion | flops 331776 | bytes 1383936 | tf_op jit(solution)/shard_map/scatter-add | solution.py:56
  5.2 0.1 reshape.49
  5.4 1.0 %convolution_bitcast_fusion.2 = f32[64,48,2,6]{0,1,3,2:T(8,128)S(1)} fusion(f32[768,2,64,1]{0,2,3,1:T(8,128)S(1)} %bitcast.68, f32[48,6,768]{2,1,0:T(8,128)S(1)} %reshape.49), kind=kOutput, calls=%fused_computation.13 | convolution fusion | flops 339738624 | bytes 1425408 | tf_op jit(solution)/shard_map/yzn,nck->kycz/dot_general | solution.py:59
  6.4 0.1 copy.26
  6.5 0.8 copy.27
  7.4 14.8 %all-to-all-start = ((f32[64,1,576]{2,1,0:T(1,128)}), f32[64,1,576]{2,1,0:T(1,128)S(1)}, u32[]{:S(2)}, u32[]{:S(2)}) async-start(f32[64,1,576]{2,1,0:T(1,128)} %copy.27), calls=%async_computation | async-start | bytes 327680 | tf_op jit(solution)/shard_map/all_to_all | solution.py:61
  22.2 4.7 %fusion.4 = (f32[384,768]{1,0:T(8,128)S(1)}, f32[384,768]{1,0:T(8,128)S(1)}) fusion(), kind=kLoop, calls=%fused_computation.9 | loop fusion | flops 2654208 | bytes 2359296 | tf_op jit(solution)/shard_map/sin | solution.py:20
  27.0 4.5 %fusion.9 = f32[384,768]{1,0:T(8,128)S(1)} fusion(), kind=kLoop, calls=%fused_computation.16 | loop fusion | flops 2949120 | bytes 1179648 | tf_op jit(solution)/shard_map/neg | solution.py:25
  31.4 4.9 %fusion.30 = (f32[1536,768]{0,1:T(8,128)}, f32[768,1536]{1,0:T(8,128)}) fusion(f32[384,768]{1,0:T(8,128)S(1)} %get-tuple-element.7, f32[384,768]{1,0:T(8,128)S(1)} %get-tuple-element.6, f32[384,768]{1,0:T(8,128)S(1)} %fusion.9), kind=kLoop, calls=%fused_computation.52 | loop fusion | flops 3538944 | bytes 12976128 | tf_op jit(solution)/shard_map/dot_general | solution.py:67
  36.3 6.1 %copy.30 = f32[1536,768]{1,0:T(8,128)} copy(f32[1536,768]{0,1:T(8,128)} %get-tuple-element.2) | data formatting | bytes 9437184 | tf_op jit(solution)/shard_map/dot_general | solution.py:67
  42.4 0.0 all-to-all-done
  42.4 1.0 %copy.28 = f32[64,1,576]{0,1,2:T(1,128)S(1)} copy(f32[64,1,576]{2,1,0:T(1,128)S(1)} %all-to-all-done) | data formatting | bytes 294912 | tf_op jit(solution)/shard_map/all_to_all | solution.py:61
  43.5 0.2 copy.29
  43.8 7.0 %convolution_bitcast_fusion.1 = f32[1,48,2,768]{3,1,2,0:T(8,128)S(1)} fusion(f32[2,768,768]{2,1,0:T(8,128)} %bitcast.65, f32[48,768]{0,1:T(8,128)S(1)} %reshape.52), kind=kOutput, calls=%fused_computation.12 | convolution fusion | flops 679477248 | bytes 5160960 | tf_op jit(solution)/shard_map/dot_general | solution.py:67
  50.7 0.5 copy.32
  51.2 2.1 %reshape.71 = f32[8,1,9216]{2,1,0:T(1,128)} reshape(f32[768,1,2,48]{3,2,1,0:T(2,128)S(1)} %bitcast.67) | data formatting | bytes 589824
  53.3 6.8 %all-to-all-start.1 = ((f32[8,1,9216]{2,1,0:T(1,128)}), f32[8,1,9216]{2,1,0:T(1,128)S(1)}, u32[]{:S(2)}, u32[]{:S(2)}) async-start(f32[8,1,9216]{2,1,0:T(1,128)} %reshape.71), calls=%async_computation.1 | async-start | bytes 589824 | tf_op jit(solution)/shard_map/all_to_all | solution.py:70
  60.1 6.1 %copy.35 = f32[1536,2,384]{2,0,1:T(8,128)} copy(f32[1536,2,384]{0,2,1:T(8,128)} %bitcast.63) | data formatting | bytes 9437184 | tf_op jit(solution)/shard_map/aycq,cyd->aqd/dot_general | solution.py:73
  66.3 5.1 %all-to-all-done.1 = f32[8,1,9216]{2,1,0:T(1,128)S(1)} async-done(((f32[8,1,9216]{2,1,0:T(1,128)}), f32[8,1,9216]{2,1,0:T(1,128)S(1)}, u32[]{:S(2)}, u32[]{:S(2)}) %all-to-all-start.1) | async-done | bytes 294944 | tf_op jit(solution)/shard_map/all_to_all | solution.py:70
  71.4 0.5 broadcast.36
  71.9 1.3 %reduce = f32[8,9216]{1,0:T(8,128)S(1)} reduce(f32[8,1,9216]{2,1,0:T(1,128)S(1)} %all-to-all-done.1, f32[]{:T(128)} %broadcast.36), dimensions={1}, to_apply=%all_to_all.9.reduce_sub_computation | reduce | bytes 589828 | tf_op jit(solution)/shard_map/all_to_all | solution.py:70
  73.2 1.3 %reshape.72 = f32[768,1,2,48]{3,2,1,0:T(2,128)S(1)} reshape(f32[8,9216]{1,0:T(8,128)S(1)} %reduce) | data formatting | bytes 589824
  74.5 0.4 copy.33
  74.9 0.2 copy.34
  75.1 0.0 copy-start
  75.1 0.0 copy-start.1
  75.1 7.0 %convolution_bitcast_fusion = f32[1,96,2,768]{3,1,2,0:T(8,128)S(1)} fusion(f32[2,768,2,384]{3,1,0,2:T(8,128)} %bitcast.64, f32[384,2,96]{0,2,1:T(8,128)S(1)} %copy.34), kind=kOutput, calls=%fused_computation.3 | convolution fusion | flops 1358954496 | bytes 5603328 | tf_op jit(solution)/shard_map/aycq,cyd->aqd/dot_general | solution.py:73
  82.1 0.0 copy-done
  82.1 0.0 copy-done.1
  82.1 0.9 %add_multiply_fusion = (f32[1,96,768]{2,1,0:T(8,128)}, f32[1,96,768]{2,1,0:T(8,128)}) fusion(f32[1,96,768]{2,1,0:T(8,128)S(1)} %copy-done, f32[1,96,768]{2,1,0:T(8,128)S(1)} %copy-done.1, f32[1,96,2,768]{3,1,2,0:T(8,128)S(1)} %convolution_bitcast_fusion), kind=kLoop, calls=%fused_computation.28 | loop fusion | flops 589824 | bytes 1769472 | tf_op jit(solution)/shard_map/mul | solution.py:79
  (3 shorter events, 0.1 us)
Async XLA Ops:
  7.4 35.1 %all-to-all-start = ((f32[64,1,576]{2,1,0:T(1,128)}), f32[64,1,576]{2,1,0:T(1,128)S(1)}, u32[]{:S(2)}, u32[]{:S(2)}) async-start(f32[64,1,576]{2,1,0:T(1,128)} %copy.27), calls=%async_computation | async-start | bytes 327680 | tf_op jit(solution)/shard_map/all_to_all | solution.py:61
  53.3 18.1 %all-to-all-start.1 = ((f32[8,1,9216]{2,1,0:T(1,128)}), f32[8,1,9216]{2,1,0:T(1,128)S(1)}, u32[]{:S(2)}, u32[]{:S(2)}) async-start(f32[8,1,9216]{2,1,0:T(1,128)} %reshape.71), calls=%async_computation.1 | async-start | bytes 589824 | tf_op jit(solution)/shard_map/all_to_all | solution.py:70
  75.1 7.0 %copy-start = (f32[1,96,768]{2,1,0:T(8,128)S(1)}, f32[1,96,768]{2,1,0:T(8,128)}, u32[]{:S(2)}) copy-start(f32[1,96,768]{2,1,0:T(8,128)} %param.11) | copy-start | bytes 884740
  75.1 7.0 %copy-start.1 = (f32[1,96,768]{2,1,0:T(8,128)S(1)}, f32[1,96,768]{2,1,0:T(8,128)}, u32[]{:S(2)}) copy-start(f32[1,96,768]{2,1,0:T(8,128)} %param.10) | copy-start | bytes 884740
where the time goes:
time: 84.5 us; the launch traced here: 83 us
  starting transfers between devices  21.7 us (26%)
  other arithmetic  21 us (25%)
  local copies, waits for them, and re-layouts  19.5 us (23%)
  matrix products  14.9 us (18%)
  waiting for transfers between devices  5.1 us (6%)
    all_to_all x1, starting transfers between devices, on_device(): lax.all_to_all(x_spectrum, 'kx', split_axis=0, concat_axis=2, tiled=True)  14.8 us
    dot_general x1, matrix products, on_device(): jnp.einsum('aycq,cyd->aqd', pencils, split_table, precision=HIGHEST)  6.97 us
    dot_general x1, matrix products, on_device(): result = jnp.dot(flat_rows, wave_table, precision=HIGHEST)  6.97 us
    all_to_all x1, starting transfers between devices, on_device(): lax.all_to_all(z_spectrum, 'gy', split_axis=3, concat_axis=1, tiled=True)  6.82 us
    dot_general x2, local copies, waits for them, and re-layouts, on_device(): result = jnp.dot(flat_rows, wave_table, precision=HIGHEST)  6.56 us
    dot_general x1, local copies, waits for them, and re-layouts, on_device(): jnp.einsum('aycq,cyd->aqd', pencils, split_table, precision=HIGHEST)  6.14 us
    sin x2, other arithmetic, angle_tables(): return (jnp.cos(angles), jnp.sin(angles))  5.16 us
    all_to_all x1, waiting for transfers between devices, on_device(): lax.all_to_all(z_spectrum, 'gy', split_axis=3, concat_axis=1, tiled=True)  5.09 us
  transfers between devices with their start and end apart: 2, of which 1 were waited for; matrix products, arithmetic and copies ran while one was open for 32% of the time, Pallas kernels for 0%

commit v1 on v0

v1 whole, which is shorter than its diff:
```python
import functools
import math

import jax
import jax.numpy as jnp
import ml_dtypes
import numpy as np
from jax import lax
from jax.experimental import pallas as pl
from jax.experimental.pallas import tpu as pltpu
from jax.sharding import PartitionSpec as P

NG = 384
BLK = 64
KXW = 64
YD = 48
ZD = 6
LCAP = 144
GY = 8
LINES_HERE = YD * ZD
WAVES = 128
F32 = jnp.float32
BF16 = jnp.bfloat16


def split(table):
    high = table.astype(np.float32).astype(ml_dtypes.bfloat16)
    low = (table - high.astype(np.float64)).astype(np.float32).astype(ml_dtypes.bfloat16)
    return high, low


def angles(first, second, length):
    return 2.0 * math.pi * ((first[:, None] * second[None, :]) % length) / length


def x_tables():
    angle = angles(np.arange(NG), np.arange(KXW), 2 * NG)
    c, s = np.cos(angle), np.sin(angle)
    return split(np.block([[c, -s], [s, c]]))


def wave_tables():
    angle = angles(np.arange(64), np.arange(WAVES), WAVES)
    c, s = np.cos(angle), np.sin(angle)
    high, low = split(np.block([[c, -s], [s, c]]))
    return np.concatenate([high, high, low], axis=0)


def twiddles():
    angle = angles(np.arange(6), np.arange(WAVES), 2 * NG)
    both = np.zeros((16, WAVES), np.float32)
    both[0:6] = np.cos(angle)
    both[8:14] = np.sin(angle)
    return both


def halves(values):
    high = values.astype(BF16)
    low = (values - high.astype(F32)).astype(BF16)
    return high, low


def dot(a, b):
    return jnp.dot(a, b, preferred_element_type=F32)


def dft3(v0, v1, v2):
    s3 = math.sqrt(3.0) / 2.0
    sum_re, sum_im = v1[0] + v2[0], v1[1] + v2[1]
    dif_re, dif_im = s3 * (v1[0] - v2[0]), s3 * (v1[1] - v2[1])
    mid_re, mid_im = v0[0] - 0.5 * sum_re, v0[1] - 0.5 * sum_im
    return (
        (v0[0] + sum_re, v0[1] + sum_im),
        (mid_re + dif_im, mid_im - dif_re),
        (mid_re - dif_im, mid_im + dif_re),
    )


def dft6(v):
    s3 = math.sqrt(3.0) / 2.0
    even = dft3(v[0], v[2], v[4])
    odd = dft3(v[1], v[3], v[5])
    turned = (
        odd[0],
        (0.5 * odd[1][0] + s3 * odd[1][1], 0.5 * odd[1][1] - s3 * odd[1][0]),
        (-0.5 * odd[2][0] + s3 * odd[2][1], -0.5 * odd[2][1] - s3 * odd[2][0]),
    )
    front = [(e[0] + o[0], e[1] + o[1]) for e, o in zip(even, turned)]
    back = [(e[0] - o[0], e[1] - o[1]) for e, o in zip(even, turned)]
    return front + back


def waves(rows, table_ref):
    high, low = halves(rows)
    both = jnp.concatenate([high, low], axis=1)
    return dot(both, table_ref[0:256]) + dot(high, table_ref[256:384])


def twisted(wave_rows, rows, twiddle_ref):
    terms = []
    for u in range(6):
        re = wave_rows[u * rows : (u + 1) * rows, 0:WAVES]
        im = wave_rows[u * rows : (u + 1) * rows, WAVES : 2 * WAVES]
        if u > 0:
            c, s = twiddle_ref[u : u + 1, :], twiddle_ref[8 + u : 9 + u, :]
            re, im = re * c + im * s, im * c - re * s
        terms.append((re, im))
    return dft6(terms)


def quotient(values, divisor):
    return jnp.floor((values + 0.5) * (1.0 / divisor))


def x_body(ids, start, stop, values, high_table, low_table):
    ids = ids.astype(F32)
    y = quotient(ids, NG)
    z = ids - NG * y
    z_here = z - ZD * quotient(z, ZD)
    y_here = y - YD * quotient(y, YD)
    t = quotient(y_here, 6)
    target = z_here * YD + (y_here - 6.0 * t) * 8.0 + t
    target = jnp.where(ids < 0, -1.0, target).astype(jnp.int32)
    bounds = jnp.concatenate(
        [start.astype(F32) * BLK, stop.astype(F32) * BLK, jnp.zeros((6, LCAP), F32)], axis=0
    )
    bounds = jnp.concatenate([bounds, jnp.zeros((8, 256 - LCAP), F32)], axis=1)
    columns = bounds.T[0:LCAP].astype(jnp.int32)
    position = lax.broadcasted_iota(jnp.int32, (LCAP, NG), 1)
    inside = (position >= columns[:, 0:1]) & (position < columns[:, 1:2])
    real = jnp.where(inside, values[:, 0:NG], 0.0)
    imag = jnp.where(inside, values[:, NG : 2 * NG], 0.0)
    high, low = halves(jnp.concatenate([real, imag], axis=1))
    spectrum = dot(high, high_table) + dot(low, high_table) + dot(high, low_table)
    place = lax.broadcasted_iota(jnp.int32, (LINES_HERE, LCAP), 0)
    chosen = jnp.where(place == target, 1.0, 0.0).astype(BF16)
    high, low = halves(spectrum)
    lines = dot(chosen, high) + dot(chosen, low)
    lines = jnp.concatenate(
        [
            lines[:, 0:KXW],
            lines[:, KXW : 2 * KXW],
            jnp.zeros((640 - 2 * LINES_HERE, KXW), F32),
        ],
        axis=0,
    )
    lines = jnp.concatenate([lines, jnp.zeros((640, KXW), F32)], axis=1)
    return lines.T[0:KXW, 0 : 2 * LINES_HERE]


def x_kernel(ids_ref, start_ref, stop_ref, values_ref, high_ref, low_ref, out_ref):
    out = x_body(
        ids_ref[...], start_ref[...], stop_ref[...], values_ref[...], high_ref[...], low_ref[...]
    )
    out_ref[:, 0, :] = out


def swap_blocks(tiles, roll):
    lane = lax.broadcasted_iota(jnp.int32, tiles[0].shape, 1)
    low64 = lane < 64
    even32 = (lane // 32) % 2 == 0
    q0, q1, q2, q3 = tiles
    q0, q2 = jnp.where(low64, q0, roll(q2, 64)), jnp.where(low64, roll(q0, 64), q2)
    q1, q3 = jnp.where(low64, q1, roll(q3, 64)), jnp.where(low64, roll(q1, 64), q3)
    q0, q1 = jnp.where(even32, q0, roll(q1, 32)), jnp.where(even32, roll(q0, 96), q1)
    q2, q3 = jnp.where(even32, q2, roll(q3, 32)), jnp.where(even32, roll(q2, 96), q3)
    return q0, q1, q2, q3


def lane_roll(values, shift):
    return pltpu.roll(values, shift, 1)


def z_body(arrived, table_ref, twiddle_ref, store, roll):
    rows = jnp.concatenate([arrived, jnp.zeros((KXW, 64), F32)], axis=1)
    rows = jnp.concatenate([rows, jnp.zeros((KXW, 640), F32)], axis=0).T
    real, imag = rows[0:LINES_HERE], rows[LINES_HERE : 2 * LINES_HERE]
    spectrum = waves(real + roll(imag, 64), table_ref)
    for j, (re, im) in enumerate(twisted(spectrum, YD, twiddle_ref)):
        tiles = swap_blocks((re[0:24], re[24:48], im[0:24], im[24:48]), roll)
        for a in range(4):
            piece = 4 * j + a
            store(piece // 3, piece % 3, tiles[a])


def z_kernel(in_ref, table_ref, twiddle_ref, out_ref):
    def store(block, third, tile):
        out_ref[block, third * 24 : third * 24 + 24, :] = tile

    z_body(in_ref[:, 0, :], table_ref, twiddle_ref, store, lane_roll)


def y_body(load, table_ref, twiddle_ref, roll):
    pieces = {}
    for third in range(3):
        for e in range(3):
            rows = jnp.concatenate(
                [load(g, third * 24 + e * 8) for g in range(GY)], axis=0
            )
            flipped = jnp.concatenate([rows, roll(rows, 64)], axis=0).T
            pieces[e, third] = flipped[0:32]
            pieces[3 + e, third] = flipped[32:64]
    rows = jnp.concatenate([pieces[u, third] for u in range(6) for third in range(3)], axis=0)
    return twisted(waves(rows, table_ref), 96, twiddle_ref)


def y_kernel(in_ref, real_ref, imag_ref, table_ref, twiddle_ref, out_re_ref, out_im_ref):
    scale = float(NG) ** (-1.5)

    def load(g, row):
        return in_ref[g, row : row + 8, :]

    for j, (re, im) in enumerate(y_body(load, table_ref, twiddle_ref, lane_roll)):
        lanes = slice(WAVES * j, WAVES * (j + 1))
        s_re, s_im = real_ref[0, :, lanes], imag_ref[0, :, lanes]
        re, im = scale * re, scale * im
        out_re_ref[0, :, lanes] = s_re * re - s_im * im
        out_im_ref[0, :, lanes] = s_re * im + s_im * re


PARAMS = pltpu.CompilerParams(vmem_limit_bytes=24 * 1024 * 1024)


def on_device(line_values, line_ids, line_start, line_stop, spectrum_real, spectrum_imag):
    high_x, low_x = x_tables()
    table = jnp.asarray(wave_tables())
    twiddle = jnp.asarray(twiddles())
    sent = pl.pallas_call(
        x_kernel,
        out_shape=jax.ShapeDtypeStruct((KXW, 1, 2 * LINES_HERE), F32),
        compiler_params=PARAMS,
        name="x_lines",
    )(
        line_ids.reshape(1, LCAP),
        line_start.reshape(1, LCAP),
        line_stop.reshape(1, LCAP),
        line_values,
        jnp.asarray(high_x),
        jnp.asarray(low_x),
    )
    arrived = lax.all_to_all(sent, "kx", split_axis=0, concat_axis=0, tiled=True)
    sent = pl.pallas_call(
        z_kernel,
        out_shape=jax.ShapeDtypeStruct((GY, 72, 128), F32),
        compiler_params=PARAMS,
        name="z_rows",
    )(arrived, table, twiddle)
    arrived = lax.all_to_all(sent, "gy", split_axis=0, concat_axis=0, tiled=True)
    out = jax.ShapeDtypeStruct(spectrum_real.shape, F32)
    return pl.pallas_call(
        y_kernel,
        out_shape=(out, out),
        compiler_params=PARAMS,
        name="y_rows",
    )(arrived, spectrum_real, spectrum_imag, table, twiddle)


def solution(mesh):
    in_specs = (
        P(("kx", "gy"), None),
        P(("kx", "gy")),
        P(("kx", "gy")),
        P(("kx", "gy")),
        P("kx", "gy", None),
        P("kx", "gy", None),
    )
    out_specs = (P("kx", "gy", None), P("kx", "gy", None))
    return jax.shard_map(
        on_device, mesh=mesh, in_specs=in_specs, out_specs=out_specs, check_vma=False
    )
```

time: 84.5 us -> 53 us (0.63); the launches traced: 83 us -> 52.7 us
  blocking collectives: 0 us -> 45.3 us
  starting transfers between devices: 21.7 us -> 0 us
  other arithmetic: 21 us -> 0 us
  local copies, waits for them, and re-layouts: 19.5 us -> 3.58 us
  matrix products: 14.9 us -> 0 us
  waiting for transfers between devices: 5.1 us -> 0 us
  Pallas kernels: 0 us -> 3.15 us
    all_to_all x0 -> x2, blocking collectives: none -> 45.3 us  [the longest x1 26.5 us: on_device(): lax.all_to_all(sent, 'kx', split_axis=0, concat_axis=0, tiled=True)]
    all_to_all x2 -> x0, starting transfers between devices: 21.7 us -> none  [the longest x1 14.8 us: on_device(): lax.all_to_all(x_spectrum, 'kx', split_axis=0, concat_axis=2, tiled=True)]
    dot_general x3 -> x0, matrix products: 14.9 us -> none  [the longest x1 6.97 us: on_device(): jnp.einsum('aycq,cyd->aqd', pencils, split_table, precision=HIGHEST)]
    dot_general x3 -> x0, local copies, waits for them, and re-layouts: 12.7 us -> none  [the longest x2 6.56 us: on_device(): result = jnp.dot(flat_rows, wave_table, precision=HIGHEST)]
    sin x2 -> x0, other arithmetic: 5.16 us -> none  [angle_tables(): return (jnp.cos(angles), jnp.sin(angles))]
    all_to_all x2 -> x0, waiting for transfers between devices: 5.1 us -> none  [the longest x1 5.09 us: on_device(): lax.all_to_all(z_spectrum, 'gy', split_axis=3, concat_axis=1, tiled=True)]
    dot_general x1 -> x0, other arithmetic: 4.9 us -> none  [on_device(): result = jnp.dot(flat_rows, wave_table, precision=HIGHEST)]
    neg x2 -> x0, other arithmetic: 4.88 us -> none  [complex_table(): first_rows = jnp.concatenate([cosine, -sine_part], axis=1)]
  transfers between devices with their start and end apart: 2 -> 0, of which waited for: 1 -> 0; matrix products, arithmetic and copies ran while one was open for 32% -> 0% of each run, Pallas kernels for 0% -> 0%
where the time goes in v1:
time: 53 us; the launch traced here: 52.7 us
  blocking collectives  45.3 us (85%)
  local copies, waits for them, and re-layouts  3.58 us (7%)
  Pallas kernels  3.15 us (6%)
  between operations  0.71 us (1%)
    all_to_all x1, blocking collectives, on_device(): lax.all_to_all(sent, 'kx', split_axis=0, concat_axis=0, tiled=True)  26.5 us
    all_to_all x1, blocking collectives, on_device(): lax.all_to_all(sent, 'gy', split_axis=0, concat_axis=0, tiled=True)  18.8 us
    unnamed x20, local copies, waits for them, and re-layouts  3.58 us
    pallas_call x1, Pallas kernels, on_device(): pl.pallas_call(y_kernel, out_shape=(out, out), compiler_params=PARAMS, na...  1.53 us

profile of v1, /device:TPU:1, one launch (start us, length us, event | category | flops | bytes accessed | tf_op | source)
XLA Modules:
  0.0 52.7 jit_solution(11825439295567339294)
XLA Ops:
  0.6 0.0 copy-start.8
  0.6 0.0 copy-start.9
  0.7 0.0 copy-start.7
  0.7 0.7 %copy-done.8 = s32[144]{0:T(256)S(1)} copy-done((s32[144]{0:T(256)S(1)}, s32[144]{0:T(256)}, u32[]{:S(2)}) %copy-start.8) | copy-done | bytes 600
  1.3 0.0 copy-done.9
  1.3 0.0 copy-done.7
  1.3 0.0 copy-start.1
  1.3 1.0 %copy-done.1 = f32[144,768]{1,0:T(8,128)S(1)} copy-done((f32[144,768]{1,0:T(8,128)S(1)}, f32[144,768]{1,0:T(8,128)}, u32[]{:S(2)}) %copy-start.1) | copy-done | bytes 442392
  2.4 0.0 copy-start.4
  2.4 0.9 %copy-done.4 = bf16[768,128]{1,0:T(8,128)(2,1)S(1)} copy-done((bf16[768,128]{1,0:T(8,128)(2,1)S(1)}, bf16[768,128]{1,0:T(8,128)(2,1)}, u32[]{:S(2)}) %copy-start.4) | copy-done | bytes 196632
  3.3 0.0 copy-start.5
  3.3 0.9 %copy-done.5 = bf16[768,128]{1,0:T(8,128)(2,1)S(1)} copy-done((bf16[768,128]{1,0:T(8,128)(2,1)S(1)}, bf16[768,128]{1,0:T(8,128)(2,1)}, u32[]{:S(2)}) %copy-start.5) | copy-done | bytes 196632
  4.2 1.0 %x_lines.1 = f32[64,1,576]{2,1,0:T(1,128)S(1)} custom-call(s32[1,144]{1,0:T(1,128)S(1)} %bitcast.3, s32[1,144]{1,0:T(1,128)S(1)} %bitcast.4, s32[1,144]{1,0:T(1,128)S(1)} %bitcast.5, f32[144,768]{1,0:T(8,128)S(1)} %copy-done.1, bf16[768,128]{1,0:T(8,128)(2,1)S(1)} %copy-done.5, bf16[768,128]{1,0:T(8,128)(2,1)S(1)} %copy-done.4), custom_call_target="tpu_custom_call" | custom-call | tf_op jit(solution)/shard_map/x_lines/pallas_call | solution.py:228
  5.2 0.0 copy-start
  5.2 0.0 copy-start.6
  5.2 26.5 %all_to_all.10.in_ref = f32[64,1,576]{2,1,0:T(1,128)S(1)} all-to-all(f32[64,1,576]{2,1,0:T(1,128)S(1)} %x_lines.1), channel_id=1, replica_groups=mesh['kx'=64,'gy'=8] {'kx'}, dimensions={0} | all-to-all | bytes 294912 | tf_op jit(solution)/shard_map/all_to_all | solution.py:241
  31.7 0.0 copy-done
  31.7 0.0 copy-done.6
  31.7 0.7 %z_rows.1 = f32[8,72,128]{2,1,0:T(8,128)S(1)} custom-call(f32[64,1,576]{2,1,0:T(1,128)S(1)} %all_to_all.10.in_ref, bf16[384,256]{1,0:T(8,128)(2,1)S(1)} %copy-done, f32[16,128]{1,0:T(8,128)S(1)} %copy-done.6), custom_call_target="tpu_custom_call" | custom-call | tf_op jit(solution)/shard_map/z_rows/pallas_call | solution.py:242
  32.3 0.0 copy-start.2
  32.3 0.0 copy-start.3
  32.4 18.8 %all_to_all.11.in_ref = f32[8,72,128]{2,1,0:T(8,128)S(1)} all-to-all(f32[8,72,128]{2,1,0:T(8,128)S(1)} %z_rows.1), channel_id=1, replica_groups=mesh['kx'=64,'gy'=8] {'gy'}, dimensions={0} | all-to-all | bytes 589824 | tf_op jit(solution)/shard_map/all_to_all | solution.py:248
  51.2 0.0 copy-done.2
  51.2 0.0 copy-done.3
  51.2 1.5 %y_rows.1 = (f32[1,96,768]{2,1,0:T(8,128)}, f32[1,96,768]{2,1,0:T(8,128)}) custom-call(f32[8,72,128]{2,1,0:T(8,128)S(1)} %all_to_all.11.in_ref, f32[1,96,768]{2,1,0:T(8,128)S(1)} %copy-done.2, f32[1,96,768]{2,1,0:T(8,128)S(1)} %copy-done.3, bf16[384,256]{1,0:T(8,128)(2,1)S(1)} %copy-done, f32[16,128]{1,0:T(8,128)S(1)} %copy-done.6), custom_call_target="tpu_custom_call" | custom-call | tf_op jit(solution)/shard_map/y_rows/pallas_call | solution.py:250
Async XLA Ops:
  0.6 0.7 %copy-start.8 = (s32[144]{0:T(256)S(1)}, s32[144]{0:T(256)}, u32[]{:S(2)}) copy-start(s32[144]{0:T(256)} %param.12) | copy-start | bytes 1732
  0.6 0.7 %copy-start.9 = (s32[144]{0:T(256)S(1)}, s32[144]{0:T(256)}, u32[]{:S(2)}) copy-start(s32[144]{0:T(256)} %param.13) | copy-start | bytes 1732
  0.7 0.7 %copy-start.7 = (s32[144]{0:T(256)S(1)}, s32[144]{0:T(256)}, u32[]{:S(2)}) copy-start(s32[144]{0:T(256)} %param.11) | copy-start | bytes 1732
  1.3 1.0 %copy-start.1 = (f32[144,768]{1,0:T(8,128)S(1)}, f32[144,768]{1,0:T(8,128)}, u32[]{:S(2)}) copy-start(f32[144,768]{1,0:T(8,128)} %values_ref.1) | copy-start | bytes 1327108
  2.4 0.9 %copy-start.4 = (bf16[768,128]{1,0:T(8,128)(2,1)S(1)}, bf16[768,128]{1,0:T(8,128)(2,1)}, u32[]{:S(2)}) copy-start(bf16[768,128]{1,0:T(8,128)(2,1)} %constant.11.clone.low_ref) | copy-start | bytes 589828
  3.3 0.9 %copy-start.5 = (bf16[768,128]{1,0:T(8,128)(2,1)S(1)}, bf16[768,128]{1,0:T(8,128)(2,1)}, u32[]{:S(2)}) copy-start(bf16[768,128]{1,0:T(8,128)(2,1)} %constant.10.clone.high_ref) | copy-start | bytes 589828
  5.2 26.5 %copy-start = (bf16[384,256]{1,0:T(8,128)(2,1)S(1)}, bf16[384,256]{1,0:T(8,128)(2,1)}, u32[]{:S(2)}) copy-start(bf16[384,256]{1,0:T(8,128)(2,1)} %constant.8.clone.table_ref) | copy-start | bytes 589828
  5.2 26.5 %copy-start.6 = (f32[16,128]{1,0:T(8,128)S(1)}, f32[16,128]{1,0:T(8,128)}, u32[]{:S(2)}) copy-start(f32[16,128]{1,0:T(8,128)} %constant.9.clone.twiddle_ref) | copy-start | bytes 24580
  32.3 18.9 %copy-start.2 = (f32[1,96,768]{2,1,0:T(8,128)S(1)}, f32[1,96,768]{2,1,0:T(8,128)}, u32[]{:S(2)}) copy-start(f32[1,96,768]{2,1,0:T(8,128)} %real_ref.1) | copy-start | bytes 884740
  32.3 18.9 %copy-start.3 = (f32[1,96,768]{2,1,0:T(8,128)S(1)}, f32[1,96,768]{2,1,0:T(8,128)}, u32[]{:S(2)}) copy-start(f32[1,96,768]{2,1,0:T(8,128)} %imag_ref.1) | copy-start | bytes 884740

commit v2 on v1

--- a/solution.py
+++ b/solution.py
@@ -35,8 +35,7 @@
 
 def x_tables():
     angle = angles(np.arange(NG), np.arange(KXW), 2 * NG)
-    c, s = np.cos(angle), np.sin(angle)
-    return split(np.block([[c, -s], [s, c]]))
+    return np.concatenate([np.cos(angle), np.sin(angle)], axis=1).astype(np.float32)
 
 
 def wave_tables():
@@ -112,7 +111,7 @@
     return jnp.floor((values + 0.5) * (1.0 / divisor))
 
 
-def x_body(ids, start, stop, values, high_table, low_table):
+def columns_of(ids, start, stop):
     ids = ids.astype(F32)
     y = quotient(ids, NG)
     z = ids - NG * y
@@ -120,39 +119,66 @@
     y_here = y - YD * quotient(y, YD)
     t = quotient(y_here, 6)
     target = z_here * YD + (y_here - 6.0 * t) * 8.0 + t
-    target = jnp.where(ids < 0, -1.0, target).astype(jnp.int32)
-    bounds = jnp.concatenate(
-        [start.astype(F32) * BLK, stop.astype(F32) * BLK, jnp.zeros((6, LCAP), F32)], axis=0
-    )
-    bounds = jnp.concatenate([bounds, jnp.zeros((8, 256 - LCAP), F32)], axis=1)
-    columns = bounds.T[0:LCAP].astype(jnp.int32)
+    target = jnp.where(ids < 0, -1024.0, target)
+    rows = [start.astype(F32) * BLK, stop.astype(F32) * BLK, target]
+    rows = jnp.concatenate(rows + [jnp.zeros((5, LCAP), F32)], axis=0)
+    rows = jnp.concatenate([rows, jnp.zeros((8, 256 - LCAP), F32)], axis=1)
+    columns = rows.T[0:LCAP].astype(jnp.int32)
+    return columns[:, 0:1], columns[:, 1:2], columns[:, 2:3]
+
+
+def placements(target):
+    place = lax.broadcasted_iota(jnp.int32, (LCAP, 640), 1)
+    first = jnp.where(place == target, 1.0, 0.0).astype(BF16)
+    second = jnp.where(place == target + LINES_HERE, 1.0, 0.0).astype(BF16)
+    return first, second
+
+
+def x_body(start, stop, first, second, values, table, roll):
     position = lax.broadcasted_iota(jnp.int32, (LCAP, NG), 1)
-    inside = (position >= columns[:, 0:1]) & (position < columns[:, 1:2])
+    inside = (position >= start) & (position < stop)
     real = jnp.where(inside, values[:, 0:NG], 0.0)
     imag = jnp.where(inside, values[:, NG : 2 * NG], 0.0)
-    high, low = halves(jnp.concatenate([real, imag], axis=1))
-    spectrum = dot(high, high_table) + dot(low, high_table) + dot(high, low_table)
-    place = lax.broadcasted_iota(jnp.int32, (LINES_HERE, LCAP), 0)
-    chosen = jnp.where(place == target, 1.0, 0.0).astype(BF16)
-    high, low = halves(spectrum)
-    lines = dot(chosen, high) + dot(chosen, low)
-    lines = jnp.concatenate(
-        [
-            lines[:, 0:KXW],
-            lines[:, KXW : 2 * KXW],
-            jnp.zeros((640 - 2 * LINES_HERE, KXW), F32),
-        ],
-        axis=0,
-    )
-    lines = jnp.concatenate([lines, jnp.zeros((640, KXW), F32)], axis=1)
-    return lines.T[0:KXW, 0 : 2 * LINES_HERE]
-
-
-def x_kernel(ids_ref, start_ref, stop_ref, values_ref, high_ref, low_ref, out_ref):
-    out = x_body(
-        ids_ref[...], start_ref[...], stop_ref[...], values_ref[...], high_ref[...], low_ref[...]
-    )
-    out_ref[:, 0, :] = out
+    high, low = halves(jnp.concatenate([real, imag], axis=0))
+    high_table, low_table = halves(table)
+    sums = dot(high, high_table) + dot(low, high_table) + dot(high, low_table)
+    lane = lax.broadcasted_iota(jnp.int32, (LCAP, 2 * KXW), 1)
+    real = sums[0:LCAP]
+    spectrum = jnp.where(lane < KXW, real, -real) + roll(sums[LCAP : 2 * LCAP], KXW)
+    spectrum = jnp.concatenate([spectrum, jnp.zeros((256 - LCAP, 2 * KXW), F32)], axis=0)
+    high, low = halves(spectrum.T[:, 0:LCAP])
+    real = jnp.concatenate([high[0:KXW], low[0:KXW]], axis=0)
+    imag = jnp.concatenate([high[KXW : 2 * KXW], low[KXW : 2 * KXW]], axis=0)
+    placed = dot(real, first) + dot(imag, second)
+    return (placed[0:KXW] + placed[KXW : 2 * KXW])[:, 0 : 2 * LINES_HERE]
+
+
+def x_kernel(
+    ids_hbm, start_hbm, stop_hbm, values_hbm, table_hbm, out_ref,
+    ids_ref, start_ref, stop_ref, values_ref, table_ref, sems,
+):
+    pairs = [
+        (ids_hbm, ids_ref),
+        (start_hbm, start_ref),
+        (stop_hbm, stop_ref),
+        (values_hbm, values_ref),
+        (table_hbm, table_ref),
+    ]
+    copies = [
+        pltpu.make_async_copy(source, target, sems.at[i])
+        for i, (source, target) in enumerate(pairs)
+    ]
+    for copy in copies:
+        copy.start()
+    for copy in copies[0:3]:
+        copy.wait()
+    start, stop, target = columns_of(ids_ref[...], start_ref[...], stop_ref[...])
+    first, second = placements(target)
+    copies[4].wait()
+    copies[3].wait()
+    out_ref[:, 0, :] = x_body(
+        start, stop, first, second, values_ref[...], table_ref[...], lane_roll
+    )
 
 
 def swap_blocks(tiles, roll):
@@ -190,53 +216,79 @@
     z_body(in_ref[:, 0, :], table_ref, twiddle_ref, store, lane_roll)
 
 
-def y_body(load, table_ref, twiddle_ref, roll):
+def y_third(load, third, table_ref, twiddle_ref, roll):
     pieces = {}
-    for third in range(3):
-        for e in range(3):
-            rows = jnp.concatenate(
-                [load(g, third * 24 + e * 8) for g in range(GY)], axis=0
-            )
-            flipped = jnp.concatenate([rows, roll(rows, 64)], axis=0).T
-            pieces[e, third] = flipped[0:32]
-            pieces[3 + e, third] = flipped[32:64]
-    rows = jnp.concatenate([pieces[u, third] for u in range(6) for third in range(3)], axis=0)
-    return twisted(waves(rows, table_ref), 96, twiddle_ref)
-
-
-def y_kernel(in_ref, real_ref, imag_ref, table_ref, twiddle_ref, out_re_ref, out_im_ref):
+    for e in range(3):
+        rows = jnp.concatenate([load(g, third * 24 + e * 8) for g in range(GY)], axis=0)
+        flipped = jnp.concatenate([rows, roll(rows, 64)], axis=0).T
+        pieces[e] = flipped[0:32]
+        pieces[3 + e] = flipped[32:64]
+    rows = jnp.concatenate([pieces[u] for u in range(6)], axis=0)
+    return twisted(waves(rows, table_ref), 32, twiddle_ref)
+
+
+def y_kernel(
+    in_ref, real_ref, imag_ref, table_ref, twiddle_ref, out_re_hbm, out_im_hbm,
+    out_re_ref, out_im_ref, sems,
+):
     scale = float(NG) ** (-1.5)
 
     def load(g, row):
         return in_ref[g, row : row + 8, :]
 
-    for j, (re, im) in enumerate(y_body(load, table_ref, twiddle_ref, lane_roll)):
-        lanes = slice(WAVES * j, WAVES * (j + 1))
-        s_re, s_im = real_ref[0, :, lanes], imag_ref[0, :, lanes]
-        re, im = scale * re, scale * im
-        out_re_ref[0, :, lanes] = s_re * re - s_im * im
-        out_im_ref[0, :, lanes] = s_re * im + s_im * re
+    copies = []
+    for third in range(3):
+        rows = slice(32 * third, 32 * third + 32)
+        for j, (re, im) in enumerate(y_third(load, third, table_ref, twiddle_ref, lane_roll)):
+            lanes = slice(WAVES * j, WAVES * (j + 1))
+            s_re, s_im = real_ref[0, rows, lanes], imag_ref[0, rows, lanes]
+            re, im = scale * re, scale * im
+            out_re_ref[0, rows, lanes] = s_re * re - s_im * im
+            out_im_ref[0, rows, lanes] = s_re * im + s_im * re
+        for i, (source, target) in enumerate(((out_re_ref, out_re_hbm), (out_im_ref, out_im_hbm))):
+            copies.append(
+                pltpu.make_async_copy(
+                    source.at[:, rows, :], target.at[:, rows, :], sems.at[2 * third + i]
+                )
+            )
+            copies[-1].start()
+    for copy in copies:
+        copy.wait()
 
 
 PARAMS = pltpu.CompilerParams(vmem_limit_bytes=24 * 1024 * 1024)
 
 
+def in_hbm(array):
+    return pltpu.with_memory_space_constraint(array, pltpu.HBM)
+
+
 def on_device(line_values, line_ids, line_start, line_stop, spectrum_real, spectrum_imag):
-    high_x, low_x = x_tables()
     table = jnp.asarray(wave_tables())
     twiddle = jnp.asarray(twiddles())
+    hbm = pl.BlockSpec(memory_space=pltpu.HBM)
+    vmem = pl.BlockSpec(memory_space=pltpu.VMEM)
     sent = pl.pallas_call(
         x_kernel,
         out_shape=jax.ShapeDtypeStruct((KXW, 1, 2 * LINES_HERE), F32),
+        in_specs=[hbm] * 5,
+        out_specs=vmem,
+        scratch_shapes=[
+            pltpu.VMEM((1, LCAP), jnp.int32),
+            pltpu.VMEM((1, LCAP), jnp.int32),
+            pltpu.VMEM((1, LCAP), jnp.int32),
+            pltpu.VMEM((LCAP, 2 * NG), F32),
+            pltpu.VMEM((NG, 2 * KXW), F32),
+            pltpu.SemaphoreType.DMA((5,)),
+        ],
         compiler_params=PARAMS,
         name="x_lines",
     )(
-        line_ids.reshape(1, LCAP),
-        line_start.reshape(1, LCAP),
-        line_stop.reshape(1, LCAP),
-        line_values,
-        jnp.asarray(high_x),
-        jnp.asarray(low_x),
+        in_hbm(line_ids.reshape(1, LCAP)),
+        in_hbm(line_start.reshape(1, LCAP)),
+        in_hbm(line_stop.reshape(1, LCAP)),
+        in_hbm(line_values),
+        in_hbm(jnp.asarray(x_tables())),
     )
     arrived = lax.all_to_all(sent, "kx", split_axis=0, concat_axis=0, tiled=True)
     sent = pl.pallas_call(
@@ -250,6 +302,13 @@
     return pl.pallas_call(
         y_kernel,
         out_shape=(out, out),
+        in_specs=[vmem] * 5,
+        out_specs=(hbm, hbm),
+        scratch_shapes=[
+            pltpu.VMEM(spectrum_real.shape, F32),
+            pltpu.VMEM(spectrum_real.shape, F32),
+            pltpu.SemaphoreType.DMA((6,)),
+        ],
         compiler_params=PARAMS,
         name="y_rows",
     )(arrived, spectrum_real, spectrum_imag, table, twiddle)

time: 53 us -> 50.3 us (0.949)
  local copies, waits for them, and re-layouts: 3.58 us -> 0.03 us
  Pallas kernels: 3.15 us -> 4.04 us
    unnamed x20 -> x8, local copies, waits for them, and re-layouts: 3.58 us -> 0.03 us
    pallas_call x1, Pallas kernels: 0.96 us -> 2.03 us  [on_device(): pl.pallas_call(x_kernel, out_shape=jax.ShapeDtypeStruct((KXW, 1, 2 * LINE...]
where the time goes in v2:
time: 50.3 us; the launch traced here: 50.1 us
  blocking collectives  45.4 us (90%)
  Pallas kernels  4.04 us (8%)
  between operations  0.68 us (1%)
    all_to_all x1, blocking collectives, on_device(): lax.all_to_all(sent, 'kx', split_axis=0, concat_axis=0, tiled=True)  26.5 us
    all_to_all x1, blocking collectives, on_device(): lax.all_to_all(sent, 'gy', split_axis=0, concat_axis=0, tiled=True)  18.9 us
    pallas_call x1, Pallas kernels, on_device(): pl.pallas_call(x_kernel, out_shape=jax.ShapeDtypeStruct((KXW, 1, 2 * LINE...  2.03 us
    pallas_call x1, Pallas kernels, on_device(): pl.pallas_call(y_kernel, out_shape=(out, out), in_specs=[vmem] * 5, out_s...  1.35 us

profile of v2, /device:TPU:1, one launch (start us, length us, event | category | flops | bytes accessed | tf_op | source)
XLA Modules:
  0.0 50.1 jit_solution(5958821724931884300)
XLA Ops:
  0.6 2.0 %x_lines.1 = f32[64,1,576]{2,1,0:T(1,128)S(1)} custom-call(s32[1,144]{1,0:T(1,128)} %bitcast.3, s32[1,144]{1,0:T(1,128)} %bitcast.4, s32[1,144]{1,0:T(1,128)} %bitcast.5, f32[144,768]{1,0:T(8,128)} %values_hbm.1, f32[384,128]{1,0:T(8,128)} %constant.8.clone.table_hbm), custom_call_target="tpu_custom_call" | custom-call | tf_op jit(solution)/shard_map/x_lines/pallas_call | solution.py:271
  2.7 0.0 copy-start
  2.7 0.0 copy-start.3
  2.7 26.5 %all_to_all.10.in_ref = f32[64,1,576]{2,1,0:T(1,128)S(1)} all-to-all(f32[64,1,576]{2,1,0:T(1,128)S(1)} %x_lines.1), channel_id=1, replica_groups=mesh['kx'=64,'gy'=8] {'kx'}, dimensions={0} | all-to-all | bytes 294912 | tf_op jit(solution)/shard_map/all_to_all | solution.py:293
  29.1 0.0 copy-done
  29.1 0.0 copy-done.3
  29.2 0.7 %z_rows.1 = f32[8,72,128]{2,1,0:T(8,128)S(1)} custom-call(f32[64,1,576]{2,1,0:T(1,128)S(1)} %all_to_all.10.in_ref, bf16[384,256]{1,0:T(8,128)(2,1)S(1)} %copy-done, f32[16,128]{1,0:T(8,128)S(1)} %copy-done.3), custom_call_target="tpu_custom_call" | custom-call | tf_op jit(solution)/shard_map/z_rows/pallas_call | solution.py:294
  29.8 0.0 copy-start.1
  29.8 0.0 copy-start.2
  29.8 18.9 %all_to_all.11.in_ref = f32[8,72,128]{2,1,0:T(8,128)S(1)} all-to-all(f32[8,72,128]{2,1,0:T(8,128)S(1)} %z_rows.1), channel_id=1, replica_groups=mesh['kx'=64,'gy'=8] {'gy'}, dimensions={0} | all-to-all | bytes 589824 | tf_op jit(solution)/shard_map/all_to_all | solution.py:300
  48.8 0.0 copy-done.1
  48.8 0.0 copy-done.2
  48.8 1.3 %y_rows.1 = (f32[1,96,768]{2,1,0:T(8,128)}, f32[1,96,768]{2,1,0:T(8,128)}) custom-call(f32[8,72,128]{2,1,0:T(8,128)S(1)} %all_to_all.11.in_ref, f32[1,96,768]{2,1,0:T(8,128)S(1)} %copy-done.1, f32[1,96,768]{2,1,0:T(8,128)S(1)} %copy-done.2, bf16[384,256]{1,0:T(8,128)(2,1)S(1)} %copy-done, f32[16,128]{1,0:T(8,128)S(1)} %copy-done.3), custom_call_target="tpu_custom_call" | custom-call | tf_op jit(solution)/shard_map/y_rows/pallas_call | solution.py:302
Async XLA Ops:
  2.7 26.5 %copy-start = (bf16[384,256]{1,0:T(8,128)(2,1)S(1)}, bf16[384,256]{1,0:T(8,128)(2,1)}, u32[]{:S(2)}) copy-start(bf16[384,256]{1,0:T(8,128)(2,1)} %constant.6.clone.table_ref) | copy-start | bytes 589828
  2.7 26.5 %copy-start.3 = (f32[16,128]{1,0:T(8,128)S(1)}, f32[16,128]{1,0:T(8,128)}, u32[]{:S(2)}) copy-start(f32[16,128]{1,0:T(8,128)} %constant.7.clone.twiddle_ref) | copy-start | bytes 24580
  29.8 18.9 %copy-start.1 = (f32[1,96,768]{2,1,0:T(8,128)S(1)}, f32[1,96,768]{2,1,0:T(8,128)}, u32[]{:S(2)}) copy-start(f32[1,96,768]{2,1,0:T(8,128)} %real_ref.1) | copy-start | bytes 884740
  29.8 18.9 %copy-start.2 = (f32[1,96,768]{2,1,0:T(8,128)S(1)}, f32[1,96,768]{2,1,0:T(8,128)}, u32[]{:S(2)}) copy-start(f32[1,96,768]{2,1,0:T(8,128)} %imag_ref.1) | copy-start | bytes 884740

commit v3 on v2

--- a/solution.py
+++ b/solution.py
@@ -23,6 +23,24 @@
 BF16 = jnp.bfloat16
 
 
+KX_FIRST = (6, 2, 1)
+GY_FIRST = 4
+
+
+def kx_order():
+    z_first, x_first, core_first = KX_FIRST
+    return [
+        ((z + z_first) % 8) * 8 + ((x + x_first) % 4) * 2 + (core + core_first) % 2
+        for z in range(8)
+        for x in range(4)
+        for core in range(2)
+    ]
+
+
+def gy_order():
+    return [(y + GY_FIRST) % GY for y in range(GY)]
+
+
 def split(table):
     high = table.astype(np.float32).astype(ml_dtypes.bfloat16)
     low = (table - high.astype(np.float64)).astype(np.float32).astype(ml_dtypes.bfloat16)
@@ -34,12 +52,12 @@
 
 
 def x_tables():
-    angle = angles(np.arange(NG), np.arange(KXW), 2 * NG)
+    angle = angles(np.arange(NG), np.array(kx_order()), 2 * NG)
     return np.concatenate([np.cos(angle), np.sin(angle)], axis=1).astype(np.float32)
 
 
-def wave_tables():
-    angle = angles(np.arange(64), np.arange(WAVES), WAVES)
+def wave_tables(order):
+    angle = angles(np.array(order), np.arange(WAVES), WAVES)
     c, s = np.cos(angle), np.sin(angle)
     high, low = split(np.block([[c, -s], [s, c]]))
     return np.concatenate([high, high, low], axis=0)
@@ -206,7 +224,7 @@
         tiles = swap_blocks((re[0:24], re[24:48], im[0:24], im[24:48]), roll)
         for a in range(4):
             piece = 4 * j + a
-            store(piece // 3, piece % 3, tiles[a])
+            store((piece // 3 - GY_FIRST) % GY, piece % 3, tiles[a])
 
 
 def z_kernel(in_ref, table_ref, twiddle_ref, out_ref):
@@ -219,7 +237,7 @@
 def y_third(load, third, table_ref, twiddle_ref, roll):
     pieces = {}
     for e in range(3):
-        rows = jnp.concatenate([load(g, third * 24 + e * 8) for g in range(GY)], axis=0)
+        rows = jnp.concatenate([load((g - GY_FIRST) % GY, third * 24 + e * 8) for g in range(GY)], axis=0)
         flipped = jnp.concatenate([rows, roll(rows, 64)], axis=0).T
         pieces[e] = flipped[0:32]
         pieces[3 + e] = flipped[32:64]
@@ -259,12 +277,19 @@
 PARAMS = pltpu.CompilerParams(vmem_limit_bytes=24 * 1024 * 1024)
 
 
+def exchange(sent, axis, order):
+    return lax.all_to_all(
+        sent, axis, split_axis=0, concat_axis=0, tiled=True, axis_index_groups=[order]
+    )
+
+
 def in_hbm(array):
     return pltpu.with_memory_space_constraint(array, pltpu.HBM)
 
 
 def on_device(line_values, line_ids, line_start, line_stop, spectrum_real, spectrum_imag):
-    table = jnp.asarray(wave_tables())
+    z_table = jnp.asarray(wave_tables(kx_order()))
+    y_table = jnp.asarray(wave_tables(range(64)))
     twiddle = jnp.asarray(twiddles())
     hbm = pl.BlockSpec(memory_space=pltpu.HBM)
     vmem = pl.BlockSpec(memory_space=pltpu.VMEM)
@@ -290,14 +315,14 @@
         in_hbm(line_values),
         in_hbm(jnp.asarray(x_tables())),
     )
-    arrived = lax.all_to_all(sent, "kx", split_axis=0, concat_axis=0, tiled=True)
+    arrived = exchange(sent, "kx", kx_order())
     sent = pl.pallas_call(
         z_kernel,
         out_shape=jax.ShapeDtypeStruct((GY, 72, 128), F32),
         compiler_params=PARAMS,
         name="z_rows",
-    )(arrived, table, twiddle)
-    arrived = lax.all_to_all(sent, "gy", split_axis=0, concat_axis=0, tiled=True)
+    )(arrived, z_table, twiddle)
+    arrived = exchange(sent, "gy", gy_order())
     out = jax.ShapeDtypeStruct(spectrum_real.shape, F32)
     return pl.pallas_call(
         y_kernel,
@@ -311,7 +336,7 @@
         ],
         compiler_params=PARAMS,
         name="y_rows",
-    )(arrived, spectrum_real, spectrum_imag, table, twiddle)
+    )(arrived, spectrum_real, spectrum_imag, y_table, twiddle)
 
 
 def solution(mesh):

time: 50.3 us -> 42.4 us (0.84)
  blocking collectives: 45.4 us -> 37.4 us
    all_to_all x2, blocking collectives: 45.4 us -> 37.4 us  [exchange(): lax.all_to_all(sent, axis, split_axis=0, concat_axis=0, tiled=True, axis_...]
where the time goes in v3:
time: 42.4 us; the launch traced here: 42.2 us
  blocking collectives  37.4 us (88%)
  Pallas kernels  4.04 us (10%)
  between operations  0.68 us (2%)
    all_to_all x2, blocking collectives, exchange(): lax.all_to_all(sent, axis, split_axis=0, concat_axis=0, tiled=True, axis_...  37.4 us
    pallas_call x1, Pallas kernels, on_device(): pl.pallas_call(x_kernel, out_shape=jax.ShapeDtypeStruct((KXW, 1, 2 * LINE...  2.03 us
    pallas_call x1, Pallas kernels, on_device(): pl.pallas_call(y_kernel, out_shape=(out, out), in_specs=[vmem] * 5, out_s...  1.35 us

profile of v3, /device:TPU:1, one launch (start us, length us, event | category | flops | bytes accessed | tf_op | source)
XLA Modules:
  0.0 42.2 jit_solution(9279382166638067972)
XLA Ops:
  0.6 2.0 %x_lines.1 = f32[64,1,576]{2,1,0:T(1,128)S(1)} custom-call(s32[1,144]{1,0:T(1,128)} %bitcast.3, s32[1,144]{1,0:T(1,128)} %bitcast.4, s32[1,144]{1,0:T(1,128)} %bitcast.5, f32[144,768]{1,0:T(8,128)} %values_hbm.1, f32[384,128]{1,0:T(8,128)} %constant.11.clone.table_hbm), custom_call_target="tpu_custom_call" | custom-call | tf_op jit(solution)/shard_map/x_lines/pallas_call | solution.py:296
  2.7 0.0 copy-start.3
  2.7 0.0 copy-start.4
  2.7 22.3 %all_to_all.10.in_ref = f32[64,1,576]{2,1,0:T(1,128)S(1)} all-to-all(f32[64,1,576]{2,1,0:T(1,128)S(1)} %x_lines.1), channel_id=1, replica_groups={{424,416,440,432,392,384,408,400,488,480,504,496,456,448,472,464,40,32,..., dimensions={0} | all-to-all | bytes 294912 | tf_op jit(solution)/shard_map/all_to_all | solution.py:281
  25.0 0.0 copy-done.3
  25.0 0.0 copy-done.4
  25.0 0.0 copy-start.2
  25.0 0.7 %z_rows.1 = f32[8,72,128]{2,1,0:T(8,128)S(1)} custom-call(f32[64,1,576]{2,1,0:T(1,128)S(1)} %all_to_all.10.in_ref, bf16[384,256]{1,0:T(8,128)(2,1)S(1)} %copy-done.3, f32[16,128]{1,0:T(8,128)S(1)} %copy-done.4), custom_call_target="tpu_custom_call" | custom-call | tf_op jit(solution)/shard_map/z_rows/pallas_call | solution.py:319
  25.6 0.0 copy-start
  25.7 0.0 copy-start.1
  25.7 15.1 %all_to_all.11.in_ref = f32[8,72,128]{2,1,0:T(8,128)S(1)} all-to-all(f32[8,72,128]{2,1,0:T(8,128)S(1)} %z_rows.1), channel_id=1, replica_groups={{4,5,6,7,0,1,2,3},{12,13,14,15,8,9,10,11},{20,21,22,23,16,17,18,19},{28..., dimensions={0} | all-to-all | bytes 589824 | tf_op jit(solution)/shard_map/all_to_all | solution.py:281
  40.8 0.0 copy-done.2
  40.8 0.0 copy-done
  40.8 0.0 copy-done.1
  40.8 1.4 %y_rows.1 = (f32[1,96,768]{2,1,0:T(8,128)}, f32[1,96,768]{2,1,0:T(8,128)}) custom-call(f32[8,72,128]{2,1,0:T(8,128)S(1)} %all_to_all.11.in_ref, f32[1,96,768]{2,1,0:T(8,128)S(1)} %copy-done, f32[1,96,768]{2,1,0:T(8,128)S(1)} %copy-done.1, bf16[384,256]{1,0:T(8,128)(2,1)S(1)} %copy-done.2, f32[16,128]{1,0:T(8,128)S(1)} %copy-done.4), custom_call_target="tpu_custom_call" | custom-call | tf_op jit(solution)/shard_map/y_rows/pallas_call | solution.py:327
Async XLA Ops:
  2.7 22.3 %copy-start.3 = (bf16[384,256]{1,0:T(8,128)(2,1)S(1)}, bf16[384,256]{1,0:T(8,128)(2,1)}, u32[]{:S(2)}) copy-start(bf16[384,256]{1,0:T(8,128)(2,1)} %constant.8.clone.table_ref) | copy-start | bytes 589828
  2.7 22.3 %copy-start.4 = (f32[16,128]{1,0:T(8,128)S(1)}, f32[16,128]{1,0:T(8,128)}, u32[]{:S(2)}) copy-start(f32[16,128]{1,0:T(8,128)} %constant.10.clone.twiddle_ref) | copy-start | bytes 24580
  25.0 15.8 %copy-start.2 = (bf16[384,256]{1,0:T(8,128)(2,1)S(1)}, bf16[384,256]{1,0:T(8,128)(2,1)}, u32[]{:S(2)}) copy-start(bf16[384,256]{1,0:T(8,128)(2,1)} %constant.9.clone.table_ref) | copy-start | bytes 589828
  25.6 15.2 %copy-start = (f32[1,96,768]{2,1,0:T(8,128)S(1)}, f32[1,96,768]{2,1,0:T(8,128)}, u32[]{:S(2)}) copy-start(f32[1,96,768]{2,1,0:T(8,128)} %real_ref.1) | copy-start | bytes 884740
  25.7 15.2 %copy-start.1 = (f32[1,96,768]{2,1,0:T(8,128)S(1)}, f32[1,96,768]{2,1,0:T(8,128)}, u32[]{:S(2)}) copy-start(f32[1,96,768]{2,1,0:T(8,128)} %imag_ref.1) | copy-start | bytes 884740

commit v4 on v3

--- a/solution.py
+++ b/solution.py
@@ -23,22 +23,13 @@
 BF16 = jnp.bfloat16
 
 
-KX_FIRST = (6, 2, 1)
-GY_FIRST = 4
-
-
-def kx_order():
-    z_first, x_first, core_first = KX_FIRST
-    return [
-        ((z + z_first) % 8) * 8 + ((x + x_first) % 4) * 2 + (core + core_first) % 2
-        for z in range(8)
-        for x in range(4)
-        for core in range(2)
-    ]
-
-
-def gy_order():
-    return [(y + GY_FIRST) % GY for y in range(GY)]
+KX_ORDER = [
+    ((z + 7) % 8) * 8 + ((x + 2) % 4) * 2 + 1 - core
+    for z in range(8)
+    for x in range(4)
+    for core in range(2)
+]
+GY_ORDER = [(y + 5) % GY for y in range(GY)]
 
 
 def split(table):
@@ -52,8 +43,8 @@
 
 
 def x_tables():
-    angle = angles(np.arange(NG), np.array(kx_order()), 2 * NG)
-    return np.concatenate([np.cos(angle), np.sin(angle)], axis=1).astype(np.float32)
+    angle = angles(np.arange(NG), np.array(KX_ORDER), 2 * NG)
+    return np.concatenate(split(np.concatenate([np.cos(angle), np.sin(angle)], axis=1)), axis=1)
 
 
 def wave_tables(order):
@@ -129,7 +120,7 @@
     return jnp.floor((values + 0.5) * (1.0 / divisor))
 
 
-def columns_of(ids, start, stop):
+def lines_of(ids):
     ids = ids.astype(F32)
     y = quotient(ids, NG)
     z = ids - NG * y
@@ -137,38 +128,39 @@
     y_here = y - YD * quotient(y, YD)
     t = quotient(y_here, 6)
     target = z_here * YD + (y_here - 6.0 * t) * 8.0 + t
-    target = jnp.where(ids < 0, -1024.0, target)
-    rows = [start.astype(F32) * BLK, stop.astype(F32) * BLK, target]
-    rows = jnp.concatenate(rows + [jnp.zeros((5, LCAP), F32)], axis=0)
+    target = jnp.where(ids < 0, -1.0, target).astype(jnp.int32)
+    place = lax.broadcasted_iota(jnp.int32, (LINES_HERE, LCAP), 0)
+    return jnp.where(place == target, 1.0, 0.0).astype(BF16)
+
+
+def cells_of(start, stop):
+    rows = [start.astype(F32) * BLK, stop.astype(F32) * BLK, jnp.zeros((6, LCAP), F32)]
+    rows = jnp.concatenate(rows, axis=0)
     rows = jnp.concatenate([rows, jnp.zeros((8, 256 - LCAP), F32)], axis=1)
     columns = rows.T[0:LCAP].astype(jnp.int32)
-    return columns[:, 0:1], columns[:, 1:2], columns[:, 2:3]
-
-
-def placements(target):
-    place = lax.broadcasted_iota(jnp.int32, (LCAP, 640), 1)
-    first = jnp.where(place == target, 1.0, 0.0).astype(BF16)
-    second = jnp.where(place == target + LINES_HERE, 1.0, 0.0).astype(BF16)
-    return first, second
-
-
-def x_body(start, stop, first, second, values, table, roll):
+    return columns[:, 0:1], columns[:, 1:2]
+
+
+def x_body(start, stop, chosen, values, table, roll):
     position = lax.broadcasted_iota(jnp.int32, (LCAP, NG), 1)
     inside = (position >= start) & (position < stop)
     real = jnp.where(inside, values[:, 0:NG], 0.0)
     imag = jnp.where(inside, values[:, NG : 2 * NG], 0.0)
     high, low = halves(jnp.concatenate([real, imag], axis=0))
-    high_table, low_table = halves(table)
-    sums = dot(high, high_table) + dot(low, high_table) + dot(high, low_table)
+    sums = dot(jnp.concatenate([high, low], axis=0), table)
+    sums = sums[:, 0 : 2 * KXW] + sums[:, 2 * KXW : 4 * KXW]
+    sums = sums[0 : 2 * LCAP] + sums[2 * LCAP : 4 * LCAP]
     lane = lax.broadcasted_iota(jnp.int32, (LCAP, 2 * KXW), 1)
     real = sums[0:LCAP]
     spectrum = jnp.where(lane < KXW, real, -real) + roll(sums[LCAP : 2 * LCAP], KXW)
-    spectrum = jnp.concatenate([spectrum, jnp.zeros((256 - LCAP, 2 * KXW), F32)], axis=0)
-    high, low = halves(spectrum.T[:, 0:LCAP])
-    real = jnp.concatenate([high[0:KXW], low[0:KXW]], axis=0)
-    imag = jnp.concatenate([high[KXW : 2 * KXW], low[KXW : 2 * KXW]], axis=0)
-    placed = dot(real, first) + dot(imag, second)
-    return (placed[0:KXW] + placed[KXW : 2 * KXW])[:, 0 : 2 * LINES_HERE]
+    placed = dot(chosen, jnp.concatenate(halves(spectrum), axis=1))
+    placed = placed[:, 0 : 2 * KXW] + placed[:, 2 * KXW : 4 * KXW]
+    placed = jnp.concatenate([placed, jnp.zeros((384 - LINES_HERE, 2 * KXW), F32)], axis=0).T
+    real, imag = placed[0:KXW], roll(placed[KXW : 2 * KXW], LINES_HERE - 256)
+    lane = lax.broadcasted_iota(jnp.int32, (KXW, 128), 1)
+    middle = jnp.where(lane < LINES_HERE - 256, real[:, 256:384], imag[:, 0:128])
+    words = [real[:, 0:256], middle, imag[:, 128 : 2 * LINES_HERE - 256]]
+    return jnp.concatenate(words, axis=1)
 
 
 def x_kernel(
@@ -190,12 +182,12 @@
         copy.start()
     for copy in copies[0:3]:
         copy.wait()
-    start, stop, target = columns_of(ids_ref[...], start_ref[...], stop_ref[...])
-    first, second = placements(target)
+    chosen = lines_of(ids_ref[...])
+    start, stop = cells_of(start_ref[...], stop_ref[...])
     copies[4].wait()
     copies[3].wait()
     out_ref[:, 0, :] = x_body(
-        start, stop, first, second, values_ref[...], table_ref[...], lane_roll
+        start, stop, chosen, values_ref[...], table_ref[...], lane_roll
     )
 
 
@@ -224,7 +216,7 @@
         tiles = swap_blocks((re[0:24], re[24:48], im[0:24], im[24:48]), roll)
         for a in range(4):
             piece = 4 * j + a
-            store((piece // 3 - GY_FIRST) % GY, piece % 3, tiles[a])
+            store(GY_ORDER.index(piece // 3), piece % 3, tiles[a])
 
 
 def z_kernel(in_ref, table_ref, twiddle_ref, out_ref):
@@ -237,7 +229,7 @@
 def y_third(load, third, table_ref, twiddle_ref, roll):
     pieces = {}
     for e in range(3):
-        rows = jnp.concatenate([load((g - GY_FIRST) % GY, third * 24 + e * 8) for g in range(GY)], axis=0)
+        rows = jnp.concatenate([load(GY_ORDER.index(g), third * 24 + e * 8) for g in range(GY)], axis=0)
         flipped = jnp.concatenate([rows, roll(rows, 64)], axis=0).T
         pieces[e] = flipped[0:32]
         pieces[3 + e] = flipped[32:64]
@@ -288,7 +280,7 @@
 
 
 def on_device(line_values, line_ids, line_start, line_stop, spectrum_real, spectrum_imag):
-    z_table = jnp.asarray(wave_tables(kx_order()))
+    z_table = jnp.asarray(wave_tables(KX_ORDER))
     y_table = jnp.asarray(wave_tables(range(64)))
     twiddle = jnp.asarray(twiddles())
     hbm = pl.BlockSpec(memory_space=pltpu.HBM)
@@ -303,7 +295,7 @@
             pltpu.VMEM((1, LCAP), jnp.int32),
             pltpu.VMEM((1, LCAP), jnp.int32),
             pltpu.VMEM((LCAP, 2 * NG), F32),
-            pltpu.VMEM((NG, 2 * KXW), F32),
+            pltpu.VMEM((NG, 4 * KXW), BF16),
             pltpu.SemaphoreType.DMA((5,)),
         ],
         compiler_params=PARAMS,
@@ -315,14 +307,14 @@
         in_hbm(line_values),
         in_hbm(jnp.asarray(x_tables())),
     )
-    arrived = exchange(sent, "kx", kx_order())
+    arrived = exchange(sent, "kx", KX_ORDER)
     sent = pl.pallas_call(
         z_kernel,
         out_shape=jax.ShapeDtypeStruct((GY, 72, 128), F32),
         compiler_params=PARAMS,
         name="z_rows",
     )(arrived, z_table, twiddle)
-    arrived = exchange(sent, "gy", gy_order())
+    arrived = exchange(sent, "gy", GY_ORDER)
     out = jax.ShapeDtypeStruct(spectrum_real.shape, F32)
     return pl.pallas_call(
         y_kernel,

time: 42.4 us -> 42 us (level)
    all_to_all x2, blocking collectives: 37.4 us -> 37 us  [exchange(): lax.all_to_all(sent, axis, split_axis=0, concat_axis=0, tiled=True, axis_...]
where the time goes in v4:
time: 42 us; the launch traced here: 41.7 us
  blocking collectives  37 us (88%)
  Pallas kernels  3.99 us (10%)
  between operations  0.68 us (2%)
    all_to_all x2, blocking collectives, exchange(): lax.all_to_all(sent, axis, split_axis=0, concat_axis=0, tiled=True, axis_...  37 us
    pallas_call x1, Pallas kernels, on_device(): pl.pallas_call(x_kernel, out_shape=jax.ShapeDtypeStruct((KXW, 1, 2 * LINE...  1.98 us
    pallas_call x1, Pallas kernels, on_device(): pl.pallas_call(y_kernel, out_shape=(out, out), in_specs=[vmem] * 5, out_s...  1.35 us

profile of v4, /device:TPU:1, one launch (start us, length us, event | category | flops | bytes accessed | tf_op | source)
XLA Modules:
  0.0 41.7 jit_solution(9123888954649240310)
XLA Ops:
  0.6 2.0 %x_lines.1 = f32[64,1,576]{2,1,0:T(1,128)S(1)} custom-call(s32[1,144]{1,0:T(1,128)} %bitcast.3, s32[1,144]{1,0:T(1,128)} %bitcast.4, s32[1,144]{1,0:T(1,128)} %bitcast.5, f32[144,768]{1,0:T(8,128)} %values_hbm.1, bf16[384,256]{1,0:T(8,128)(2,1)} %constant.11.clone.table_hbm), custom_call_target="tpu_custom_call" | custom-call | tf_op jit(solution)/shard_map/x_lines/pallas_call | solution.py:288
  2.6 0.0 copy-start.3
  2.6 0.0 copy-start.4
  2.6 22.4 %all_to_all.10.in_ref = f32[64,1,576]{2,1,0:T(1,128)S(1)} all-to-all(f32[64,1,576]{2,1,0:T(1,128)S(1)} %x_lines.1), channel_id=1, replica_groups={{488,480,504,496,456,448,472,464,40,32,56,48,8,0,24,16,104,96,120,112,7..., dimensions={0} | all-to-all | bytes 294912 | tf_op jit(solution)/shard_map/all_to_all | solution.py:273
  25.0 0.0 copy-done.3
  25.0 0.0 copy-done.4
  25.0 0.0 copy-start.2
  25.0 0.7 %z_rows.1 = f32[8,72,128]{2,1,0:T(8,128)S(1)} custom-call(f32[64,1,576]{2,1,0:T(1,128)S(1)} %all_to_all.10.in_ref, bf16[384,256]{1,0:T(8,128)(2,1)S(1)} %copy-done.3, f32[16,128]{1,0:T(8,128)S(1)} %copy-done.4), custom_call_target="tpu_custom_call" | custom-call | tf_op jit(solution)/shard_map/z_rows/pallas_call | solution.py:311
  25.7 0.0 copy-start
  25.7 0.0 copy-start.1
  25.7 14.6 %all_to_all.11.in_ref = f32[8,72,128]{2,1,0:T(8,128)S(1)} all-to-all(f32[8,72,128]{2,1,0:T(8,128)S(1)} %z_rows.1), channel_id=1, replica_groups={{5,6,7,0,1,2,3,4},{13,14,15,8,9,10,11,12},{21,22,23,16,17,18,19,20},{29..., dimensions={0} | all-to-all | bytes 589824 | tf_op jit(solution)/shard_map/all_to_all | solution.py:273
  40.3 0.0 copy-done.2
  40.3 0.0 copy-done
  40.3 0.0 copy-done.1
  40.3 1.4 %y_rows.1 = (f32[1,96,768]{2,1,0:T(8,128)}, f32[1,96,768]{2,1,0:T(8,128)}) custom-call(f32[8,72,128]{2,1,0:T(8,128)S(1)} %all_to_all.11.in_ref, f32[1,96,768]{2,1,0:T(8,128)S(1)} %copy-done, f32[1,96,768]{2,1,0:T(8,128)S(1)} %copy-done.1, bf16[384,256]{1,0:T(8,128)(2,1)S(1)} %copy-done.2, f32[16,128]{1,0:T(8,128)S(1)} %copy-done.4), custom_call_target="tpu_custom_call" | custom-call | tf_op jit(solution)/shard_map/y_rows/pallas_call | solution.py:319
Async XLA Ops:
  2.6 22.4 %copy-start.3 = (bf16[384,256]{1,0:T(8,128)(2,1)S(1)}, bf16[384,256]{1,0:T(8,128)(2,1)}, u32[]{:S(2)}) copy-start(bf16[384,256]{1,0:T(8,128)(2,1)} %constant.8.clone.table_ref) | copy-start | bytes 589828
  2.6 22.4 %copy-start.4 = (f32[16,128]{1,0:T(8,128)S(1)}, f32[16,128]{1,0:T(8,128)}, u32[]{:S(2)}) copy-start(f32[16,128]{1,0:T(8,128)} %constant.10.clone.twiddle_ref) | copy-start | bytes 24580
  25.0 15.3 %copy-start.2 = (bf16[384,256]{1,0:T(8,128)(2,1)S(1)}, bf16[384,256]{1,0:T(8,128)(2,1)}, u32[]{:S(2)}) copy-start(bf16[384,256]{1,0:T(8,128)(2,1)} %constant.9.clone.table_ref) | copy-start | bytes 589828
  25.7 14.6 %copy-start = (f32[1,96,768]{2,1,0:T(8,128)S(1)}, f32[1,96,768]{2,1,0:T(8,128)}, u32[]{:S(2)}) copy-start(f32[1,96,768]{2,1,0:T(8,128)} %real_ref.1) | copy-start | bytes 884740
  25.7 14.6 %copy-start.1 = (f32[1,96,768]{2,1,0:T(8,128)S(1)}, f32[1,96,768]{2,1,0:T(8,128)}, u32[]{:S(2)}) copy-start(f32[1,96,768]{2,1,0:T(8,128)} %imag_ref.1) | copy-start | bytes 884740

commit v5 on v4

--- a/solution.py
+++ b/solution.py
@@ -156,11 +156,11 @@
     placed = dot(chosen, jnp.concatenate(halves(spectrum), axis=1))
     placed = placed[:, 0 : 2 * KXW] + placed[:, 2 * KXW : 4 * KXW]
     placed = jnp.concatenate([placed, jnp.zeros((384 - LINES_HERE, 2 * KXW), F32)], axis=0).T
-    real, imag = placed[0:KXW], roll(placed[KXW : 2 * KXW], LINES_HERE - 256)
+    real, imag = placed[0:KXW], placed[KXW : 2 * KXW]
+    rest = LINES_HERE - 256
     lane = lax.broadcasted_iota(jnp.int32, (KXW, 128), 1)
-    middle = jnp.where(lane < LINES_HERE - 256, real[:, 256:384], imag[:, 0:128])
-    words = [real[:, 0:256], middle, imag[:, 128 : 2 * LINES_HERE - 256]]
-    return jnp.concatenate(words, axis=1)
+    last = jnp.where(lane < rest, real[:, 256:384], roll(imag[:, 256:384], rest))
+    return jnp.concatenate([real[:, 0:256], imag[:, 0:256], last[:, 0 : 2 * rest]], axis=1)
 
 
 def x_kernel(
@@ -208,10 +208,13 @@
 
 
 def z_body(arrived, table_ref, twiddle_ref, store, roll):
-    rows = jnp.concatenate([arrived, jnp.zeros((KXW, 64), F32)], axis=1)
-    rows = jnp.concatenate([rows, jnp.zeros((KXW, 640), F32)], axis=0).T
-    real, imag = rows[0:LINES_HERE], rows[LINES_HERE : 2 * LINES_HERE]
-    spectrum = waves(real + roll(imag, 64), table_ref)
+    rest = LINES_HERE - 256
+    last = jnp.concatenate([arrived[:, 512:576], jnp.zeros((KXW, 64), F32)], axis=1)
+    real = [arrived[:, 0:128], arrived[:, 128:256], last]
+    imag = [arrived[:, 256:384], arrived[:, 384:512], roll(last, 128 - rest)]
+    rows = [jnp.concatenate(pair, axis=0).T for pair in zip(real, imag)]
+    rows = jnp.concatenate([rows[0], rows[1], rows[2][0:rest]], axis=0)
+    spectrum = waves(rows, table_ref)
     for j, (re, im) in enumerate(twisted(spectrum, YD, twiddle_ref)):
         tiles = swap_blocks((re[0:24], re[24:48], im[0:24], im[24:48]), roll)
         for a in range(4):
@@ -226,15 +229,16 @@
     z_body(in_ref[:, 0, :], table_ref, twiddle_ref, store, lane_roll)
 
 
-def y_third(load, third, table_ref, twiddle_ref, roll):
+def y_waves(load, third, table_ref, roll):
     pieces = {}
     for e in range(3):
-        rows = jnp.concatenate([load(GY_ORDER.index(g), third * 24 + e * 8) for g in range(GY)], axis=0)
+        rows = jnp.concatenate(
+            [load(GY_ORDER.index(g), third * 24 + e * 8) for g in range(GY)], axis=0
+        )
         flipped = jnp.concatenate([rows, roll(rows, 64)], axis=0).T
         pieces[e] = flipped[0:32]
         pieces[3 + e] = flipped[32:64]
-    rows = jnp.concatenate([pieces[u] for u in range(6)], axis=0)
-    return twisted(waves(rows, table_ref), 32, twiddle_ref)
+    return waves(jnp.concatenate([pieces[u] for u in range(6)], axis=0), table_ref)
 
 
 def y_kernel(
@@ -247,9 +251,13 @@
         return in_ref[g, row : row + 8, :]
 
     copies = []
+    spectrum = y_waves(load, 0, table_ref, lane_roll)
     for third in range(3):
         rows = slice(32 * third, 32 * third + 32)
-        for j, (re, im) in enumerate(y_third(load, third, table_ref, twiddle_ref, lane_roll)):
+        here = spectrum
+        if third < 2:
+            spectrum = y_waves(load, third + 1, table_ref, lane_roll)
+        for j, (re, im) in enumerate(twisted(here, 32, twiddle_ref)):
             lanes = slice(WAVES * j, WAVES * (j + 1))
             s_re, s_im = real_ref[0, rows, lanes], imag_ref[0, rows, lanes]
             re, im = scale * re, scale * im

time: 42 us -> 41.9 us (level)
  no operation moved by 1% of the time
where the time goes in v5:
time: 41.9 us; the launch traced here: 41.6 us
  blocking collectives  37 us (88%)
  Pallas kernels  3.86 us (9%)
  between operations  0.68 us (2%)
    all_to_all x2, blocking collectives, exchange(): lax.all_to_all(sent, axis, split_axis=0, concat_axis=0, tiled=True, axis_...  37 us
    pallas_call x1, Pallas kernels, on_device(): pl.pallas_call(x_kernel, out_shape=jax.ShapeDtypeStruct((KXW, 1, 2 * LINE...  1.98 us
    pallas_call x1, Pallas kernels, on_device(): pl.pallas_call(y_kernel, out_shape=(out, out), in_specs=[vmem] * 5, out_s...  1.35 us

profile of v5, /device:TPU:1, one launch (start us, length us, event | category | flops | bytes accessed | tf_op | source)
XLA Modules:
  0.0 41.6 jit_solution(5200736751904090991)
XLA Ops:
  0.6 2.0 %x_lines.1 = f32[64,1,576]{2,1,0:T(1,128)S(1)} custom-call(s32[1,144]{1,0:T(1,128)} %bitcast.3, s32[1,144]{1,0:T(1,128)} %bitcast.4, s32[1,144]{1,0:T(1,128)} %bitcast.5, f32[144,768]{1,0:T(8,128)} %values_hbm.1, bf16[384,256]{1,0:T(8,128)(2,1)} %constant.11.clone.table_hbm), custom_call_target="tpu_custom_call" | custom-call | tf_op jit(solution)/shard_map/x_lines/pallas_call | solution.py:296
  2.6 0.0 copy-start.3
  2.6 0.0 copy-start.4
  2.6 22.4 %all_to_all.10.in_ref = f32[64,1,576]{2,1,0:T(1,128)S(1)} all-to-all(f32[64,1,576]{2,1,0:T(1,128)S(1)} %x_lines.1), channel_id=1, replica_groups={{488,480,504,496,456,448,472,464,40,32,56,48,8,0,24,16,104,96,120,112,7..., dimensions={0} | all-to-all | bytes 294912 | tf_op jit(solution)/shard_map/all_to_all | solution.py:281
  25.0 0.0 copy-done.3
  25.0 0.0 copy-done.4
  25.0 0.0 copy-start.2
  25.0 0.5 %z_rows.1 = f32[8,72,128]{2,1,0:T(8,128)S(1)} custom-call(f32[64,1,576]{2,1,0:T(1,128)S(1)} %all_to_all.10.in_ref, bf16[384,256]{1,0:T(8,128)(2,1)S(1)} %copy-done.3, f32[16,128]{1,0:T(8,128)S(1)} %copy-done.4), custom_call_target="tpu_custom_call" | custom-call | tf_op jit(solution)/shard_map/z_rows/pallas_call | solution.py:319
  25.6 0.0 copy-start
  25.6 0.0 copy-start.1
  25.6 14.6 %all_to_all.11.in_ref = f32[8,72,128]{2,1,0:T(8,128)S(1)} all-to-all(f32[8,72,128]{2,1,0:T(8,128)S(1)} %z_rows.1), channel_id=1, replica_groups={{5,6,7,0,1,2,3,4},{13,14,15,8,9,10,11,12},{21,22,23,16,17,18,19,20},{29..., dimensions={0} | all-to-all | bytes 589824 | tf_op jit(solution)/shard_map/all_to_all | solution.py:281
  40.2 0.0 copy-done.2
  40.2 0.0 copy-done
  40.2 0.0 copy-done.1
  40.2 1.4 %y_rows.1 = (f32[1,96,768]{2,1,0:T(8,128)}, f32[1,96,768]{2,1,0:T(8,128)}) custom-call(f32[8,72,128]{2,1,0:T(8,128)S(1)} %all_to_all.11.in_ref, f32[1,96,768]{2,1,0:T(8,128)S(1)} %copy-done, f32[1,96,768]{2,1,0:T(8,128)S(1)} %copy-done.1, bf16[384,256]{1,0:T(8,128)(2,1)S(1)} %copy-done.2, f32[16,128]{1,0:T(8,128)S(1)} %copy-done.4), custom_call_target="tpu_custom_call" | custom-call | tf_op jit(solution)/shard_map/y_rows/pallas_call | solution.py:327
Async XLA Ops:
  2.6 22.4 %copy-start.3 = (bf16[384,256]{1,0:T(8,128)(2,1)S(1)}, bf16[384,256]{1,0:T(8,128)(2,1)}, u32[]{:S(2)}) copy-start(bf16[384,256]{1,0:T(8,128)(2,1)} %constant.8.clone.table_ref) | copy-start | bytes 589828
  2.6 22.4 %copy-start.4 = (f32[16,128]{1,0:T(8,128)S(1)}, f32[16,128]{1,0:T(8,128)}, u32[]{:S(2)}) copy-start(f32[16,128]{1,0:T(8,128)} %constant.10.clone.twiddle_ref) | copy-start | bytes 24580
  25.0 15.2 %copy-start.2 = (bf16[384,256]{1,0:T(8,128)(2,1)S(1)}, bf16[384,256]{1,0:T(8,128)(2,1)}, u32[]{:S(2)}) copy-start(bf16[384,256]{1,0:T(8,128)(2,1)} %constant.9.clone.table_ref) | copy-start | bytes 589828
  25.6 14.6 %copy-start = (f32[1,96,768]{2,1,0:T(8,128)S(1)}, f32[1,96,768]{2,1,0:T(8,128)}, u32[]{:S(2)}) copy-start(f32[1,96,768]{2,1,0:T(8,128)} %real_ref.1) | copy-start | bytes 884740
  25.6 14.6 %copy-start.1 = (f32[1,96,768]{2,1,0:T(8,128)S(1)}, f32[1,96,768]{2,1,0:T(8,128)}, u32[]{:S(2)}) copy-start(f32[1,96,768]{2,1,0:T(8,128)} %imag_ref.1) | copy-start | bytes 884740

commit v6 on v5

--- a/solution.py
+++ b/solution.py
@@ -47,9 +47,9 @@
     return np.concatenate(split(np.concatenate([np.cos(angle), np.sin(angle)], axis=1)), axis=1)
 
 
-def wave_tables(order):
+def wave_tables(order, scale=1.0):
     angle = angles(np.array(order), np.arange(WAVES), WAVES)
-    c, s = np.cos(angle), np.sin(angle)
+    c, s = scale * np.cos(angle), scale * np.sin(angle)
     high, low = split(np.block([[c, -s], [s, c]]))
     return np.concatenate([high, high, low], axis=0)
 
@@ -168,11 +168,11 @@
     ids_ref, start_ref, stop_ref, values_ref, table_ref, sems,
 ):
     pairs = [
+        (values_hbm, values_ref),
+        (table_hbm, table_ref),
         (ids_hbm, ids_ref),
         (start_hbm, start_ref),
         (stop_hbm, stop_ref),
-        (values_hbm, values_ref),
-        (table_hbm, table_ref),
     ]
     copies = [
         pltpu.make_async_copy(source, target, sems.at[i])
@@ -180,12 +180,12 @@
     ]
     for copy in copies:
         copy.start()
-    for copy in copies[0:3]:
+    for copy in copies[2:5]:
         copy.wait()
     chosen = lines_of(ids_ref[...])
     start, stop = cells_of(start_ref[...], stop_ref[...])
-    copies[4].wait()
-    copies[3].wait()
+    copies[1].wait()
+    copies[0].wait()
     out_ref[:, 0, :] = x_body(
         start, stop, chosen, values_ref[...], table_ref[...], lane_roll
     )
@@ -245,8 +245,6 @@
     in_ref, real_ref, imag_ref, table_ref, twiddle_ref, out_re_hbm, out_im_hbm,
     out_re_ref, out_im_ref, sems,
 ):
-    scale = float(NG) ** (-1.5)
-
     def load(g, row):
         return in_ref[g, row : row + 8, :]
 
@@ -260,7 +258,6 @@
         for j, (re, im) in enumerate(twisted(here, 32, twiddle_ref)):
             lanes = slice(WAVES * j, WAVES * (j + 1))
             s_re, s_im = real_ref[0, rows, lanes], imag_ref[0, rows, lanes]
-            re, im = scale * re, scale * im
             out_re_ref[0, rows, lanes] = s_re * re - s_im * im
             out_im_ref[0, rows, lanes] = s_re * im + s_im * re
         for i, (source, target) in enumerate(((out_re_ref, out_re_hbm), (out_im_ref, out_im_hbm))):
@@ -289,7 +286,7 @@
 
 def on_device(line_values, line_ids, line_start, line_stop, spectrum_real, spectrum_imag):
     z_table = jnp.asarray(wave_tables(KX_ORDER))
-    y_table = jnp.asarray(wave_tables(range(64)))
+    y_table = jnp.asarray(wave_tables(range(64), float(NG) ** (-1.5)))
     twiddle = jnp.asarray(twiddles())
     hbm = pl.BlockSpec(memory_space=pltpu.HBM)
     vmem = pl.BlockSpec(memory_space=pltpu.VMEM)

time: 41.9 us -> 41.8 us (level)
  no operation moved by 1% of the time
where the time goes in v6:
time: 41.8 us; the launch traced here: 41.5 us
  blocking collectives  37 us (89%)
  Pallas kernels  3.8 us (9%)
  between operations  0.68 us (2%)
    all_to_all x2, blocking collectives, exchange(): lax.all_to_all(sent, axis, split_axis=0, concat_axis=0, tiled=True, axis_...  37 us
    pallas_call x1, Pallas kernels, on_device(): pl.pallas_call(x_kernel, out_shape=jax.ShapeDtypeStruct((KXW, 1, 2 * LINE...  1.93 us
    pallas_call x1, Pallas kernels, on_device(): pl.pallas_call(y_kernel, out_shape=(out, out), in_specs=[vmem] * 5, out_s...  1.33 us

profile of v6, /device:TPU:1, one launch (start us, length us, event | category | flops | bytes accessed | tf_op | source)
XLA Modules:
  0.0 41.5 jit_solution(15405538327244870430)
XLA Ops:
  0.6 1.9 %x_lines.1 = f32[64,1,576]{2,1,0:T(1,128)S(1)} custom-call(s32[1,144]{1,0:T(1,128)} %bitcast.3, s32[1,144]{1,0:T(1,128)} %bitcast.4, s32[1,144]{1,0:T(1,128)} %bitcast.5, f32[144,768]{1,0:T(8,128)} %values_hbm.1, bf16[384,256]{1,0:T(8,128)(2,1)} %constant.11.clone.table_hbm), custom_call_target="tpu_custom_call" | custom-call | tf_op jit(solution)/shard_map/x_lines/pallas_call | solution.py:293
  2.6 0.0 copy-start.3
  2.6 0.0 copy-start.4
  2.6 22.4 %all_to_all.10.in_ref = f32[64,1,576]{2,1,0:T(1,128)S(1)} all-to-all(f32[64,1,576]{2,1,0:T(1,128)S(1)} %x_lines.1), channel_id=1, replica_groups={{488,480,504,496,456,448,472,464,40,32,56,48,8,0,24,16,104,96,120,112,7..., dimensions={0} | all-to-all | bytes 294912 | tf_op jit(solution)/shard_map/all_to_all | solution.py:278
  25.0 0.0 copy-done.3
  25.0 0.0 copy-done.4
  25.0 0.0 copy-start.2
  25.0 0.5 %z_rows.1 = f32[8,72,128]{2,1,0:T(8,128)S(1)} custom-call(f32[64,1,576]{2,1,0:T(1,128)S(1)} %all_to_all.10.in_ref, bf16[384,256]{1,0:T(8,128)(2,1)S(1)} %copy-done.3, f32[16,128]{1,0:T(8,128)S(1)} %copy-done.4), custom_call_target="tpu_custom_call" | custom-call | tf_op jit(solution)/shard_map/z_rows/pallas_call | solution.py:316
  25.5 0.0 copy-start
  25.6 0.0 copy-start.1
  25.6 14.6 %all_to_all.11.in_ref = f32[8,72,128]{2,1,0:T(8,128)S(1)} all-to-all(f32[8,72,128]{2,1,0:T(8,128)S(1)} %z_rows.1), channel_id=1, replica_groups={{5,6,7,0,1,2,3,4},{13,14,15,8,9,10,11,12},{21,22,23,16,17,18,19,20},{29..., dimensions={0} | all-to-all | bytes 589824 | tf_op jit(solution)/shard_map/all_to_all | solution.py:278
  40.2 0.0 copy-done.2
  40.2 0.0 copy-done
  40.2 0.0 copy-done.1
  40.2 1.3 %y_rows.1 = (f32[1,96,768]{2,1,0:T(8,128)}, f32[1,96,768]{2,1,0:T(8,128)}) custom-call(f32[8,72,128]{2,1,0:T(8,128)S(1)} %all_to_all.11.in_ref, f32[1,96,768]{2,1,0:T(8,128)S(1)} %copy-done, f32[1,96,768]{2,1,0:T(8,128)S(1)} %copy-done.1, bf16[384,256]{1,0:T(8,128)(2,1)S(1)} %copy-done.2, f32[16,128]{1,0:T(8,128)S(1)} %copy-done.4), custom_call_target="tpu_custom_call" | custom-call | tf_op jit(solution)/shard_map/y_rows/pallas_call | solution.py:324
Async XLA Ops:
  2.6 22.4 %copy-start.3 = (bf16[384,256]{1,0:T(8,128)(2,1)S(1)}, bf16[384,256]{1,0:T(8,128)(2,1)}, u32[]{:S(2)}) copy-start(bf16[384,256]{1,0:T(8,128)(2,1)} %constant.8.clone.table_ref) | copy-start | bytes 589828
  2.6 22.4 %copy-start.4 = (f32[16,128]{1,0:T(8,128)S(1)}, f32[16,128]{1,0:T(8,128)}, u32[]{:S(2)}) copy-start(f32[16,128]{1,0:T(8,128)} %constant.10.clone.twiddle_ref) | copy-start | bytes 24580
  25.0 15.2 %copy-start.2 = (bf16[384,256]{1,0:T(8,128)(2,1)S(1)}, bf16[384,256]{1,0:T(8,128)(2,1)}, u32[]{:S(2)}) copy-start(bf16[384,256]{1,0:T(8,128)(2,1)} %constant.9.clone.table_ref) | copy-start | bytes 589828
  25.5 14.6 %copy-start = (f32[1,96,768]{2,1,0:T(8,128)S(1)}, f32[1,96,768]{2,1,0:T(8,128)}, u32[]{:S(2)}) copy-start(f32[1,96,768]{2,1,0:T(8,128)} %real_ref.1) | copy-start | bytes 884740
  25.6 14.6 %copy-start.1 = (f32[1,96,768]{2,1,0:T(8,128)S(1)}, f32[1,96,768]{2,1,0:T(8,128)}, u32[]{:S(2)}) copy-start(f32[1,96,768]{2,1,0:T(8,128)} %imag_ref.1) | copy-start | bytes 884740

commit v7 on v6

--- a/solution.py
+++ b/solution.py
@@ -24,7 +24,7 @@
 
 
 KX_ORDER = [
-    ((z + 7) % 8) * 8 + ((x + 2) % 4) * 2 + 1 - core
+    ((z + 7) % 8) * 8 + ((2 - x) % 4) * 2 + 1 - core
     for z in range(8)
     for x in range(4)
     for core in range(2)
@@ -180,12 +180,12 @@
     ]
     for copy in copies:
         copy.start()
-    for copy in copies[2:5]:
+    copies[3].wait()
+    copies[4].wait()
+    start, stop = cells_of(start_ref[...], stop_ref[...])
+    for copy in copies[0:3]:
         copy.wait()
     chosen = lines_of(ids_ref[...])
-    start, stop = cells_of(start_ref[...], stop_ref[...])
-    copies[1].wait()
-    copies[0].wait()
     out_ref[:, 0, :] = x_body(
         start, stop, chosen, values_ref[...], table_ref[...], lane_roll
     )

time: 41.8 us -> 41.7 us (level)
  no operation moved by 1% of the time
where the time goes in v7:
time: 41.7 us; the launch traced here: 41.5 us
  blocking collectives  37 us (89%)
  Pallas kernels  3.8 us (9%)
  between operations  0.68 us (2%)
    all_to_all x2, blocking collectives, exchange(): lax.all_to_all(sent, axis, split_axis=0, concat_axis=0, tiled=True, axis_...  37 us
    pallas_call x1, Pallas kernels, on_device(): pl.pallas_call(x_kernel, out_shape=jax.ShapeDtypeStruct((KXW, 1, 2 * LINE...  1.93 us
    pallas_call x1, Pallas kernels, on_device(): pl.pallas_call(y_kernel, out_shape=(out, out), in_specs=[vmem] * 5, out_s...  1.34 us

profile of v7, /device:TPU:1, one launch (start us, length us, event | category | flops | bytes accessed | tf_op | source)
XLA Modules:
  0.0 41.5 jit_solution(12213297513525125550)
XLA Ops:
  0.6 1.9 %x_lines.1 = f32[64,1,576]{2,1,0:T(1,128)S(1)} custom-call(s32[1,144]{1,0:T(1,128)} %bitcast.3, s32[1,144]{1,0:T(1,128)} %bitcast.4, s32[1,144]{1,0:T(1,128)} %bitcast.5, f32[144,768]{1,0:T(8,128)} %values_hbm.1, bf16[384,256]{1,0:T(8,128)(2,1)} %constant.11.clone.table_hbm), custom_call_target="tpu_custom_call" | custom-call | tf_op jit(solution)/shard_map/x_lines/pallas_call | solution.py:293
  2.6 0.0 copy-start.3
  2.6 0.0 copy-start.4
  2.6 22.4 %all_to_all.10.in_ref = f32[64,1,576]{2,1,0:T(1,128)S(1)} all-to-all(f32[64,1,576]{2,1,0:T(1,128)S(1)} %x_lines.1), channel_id=1, replica_groups={{488,480,472,464,456,448,504,496,40,32,24,16,8,0,56,48,104,96,88,80,72,..., dimensions={0} | all-to-all | bytes 294912 | tf_op jit(solution)/shard_map/all_to_all | solution.py:278
  25.0 0.0 copy-done.3
  25.0 0.0 copy-done.4
  25.0 0.0 copy-start.2
  25.0 0.5 %z_rows.1 = f32[8,72,128]{2,1,0:T(8,128)S(1)} custom-call(f32[64,1,576]{2,1,0:T(1,128)S(1)} %all_to_all.10.in_ref, bf16[384,256]{1,0:T(8,128)(2,1)S(1)} %copy-done.3, f32[16,128]{1,0:T(8,128)S(1)} %copy-done.4), custom_call_target="tpu_custom_call" | custom-call | tf_op jit(solution)/shard_map/z_rows/pallas_call | solution.py:316
  25.5 0.0 copy-start
  25.5 0.0 copy-start.1
  25.6 14.6 %all_to_all.11.in_ref = f32[8,72,128]{2,1,0:T(8,128)S(1)} all-to-all(f32[8,72,128]{2,1,0:T(8,128)S(1)} %z_rows.1), channel_id=1, replica_groups={{5,6,7,0,1,2,3,4},{13,14,15,8,9,10,11,12},{21,22,23,16,17,18,19,20},{29..., dimensions={0} | all-to-all | bytes 589824 | tf_op jit(solution)/shard_map/all_to_all | solution.py:278
  40.1 0.0 copy-done.2
  40.2 0.0 copy-done
  40.2 0.0 copy-done.1
  40.2 1.3 %y_rows.1 = (f32[1,96,768]{2,1,0:T(8,128)}, f32[1,96,768]{2,1,0:T(8,128)}) custom-call(f32[8,72,128]{2,1,0:T(8,128)S(1)} %all_to_all.11.in_ref, f32[1,96,768]{2,1,0:T(8,128)S(1)} %copy-done, f32[1,96,768]{2,1,0:T(8,128)S(1)} %copy-done.1, bf16[384,256]{1,0:T(8,128)(2,1)S(1)} %copy-done.2, f32[16,128]{1,0:T(8,128)S(1)} %copy-done.4), custom_call_target="tpu_custom_call" | custom-call | tf_op jit(solution)/shard_map/y_rows/pallas_call | solution.py:324
Async XLA Ops:
  2.6 22.4 %copy-start.3 = (bf16[384,256]{1,0:T(8,128)(2,1)S(1)}, bf16[384,256]{1,0:T(8,128)(2,1)}, u32[]{:S(2)}) copy-start(bf16[384,256]{1,0:T(8,128)(2,1)} %constant.8.clone.table_ref) | copy-start | bytes 589828
  2.6 22.4 %copy-start.4 = (f32[16,128]{1,0:T(8,128)S(1)}, f32[16,128]{1,0:T(8,128)}, u32[]{:S(2)}) copy-start(f32[16,128]{1,0:T(8,128)} %constant.10.clone.twiddle_ref) | copy-start | bytes 24580
  25.0 15.2 %copy-start.2 = (bf16[384,256]{1,0:T(8,128)(2,1)S(1)}, bf16[384,256]{1,0:T(8,128)(2,1)}, u32[]{:S(2)}) copy-start(bf16[384,256]{1,0:T(8,128)(2,1)} %constant.9.clone.table_ref) | copy-start | bytes 589828
  25.5 14.6 %copy-start = (f32[1,96,768]{2,1,0:T(8,128)S(1)}, f32[1,96,768]{2,1,0:T(8,128)}, u32[]{:S(2)}) copy-start(f32[1,96,768]{2,1,0:T(8,128)} %real_ref.1) | copy-start | bytes 884740
  25.5 14.6 %copy-start.1 = (f32[1,96,768]{2,1,0:T(8,128)S(1)}, f32[1,96,768]{2,1,0:T(8,128)}, u32[]{:S(2)}) copy-start(f32[1,96,768]{2,1,0:T(8,128)} %imag_ref.1) | copy-start | bytes 884740

commit v8 on v7

--- a/solution.py
+++ b/solution.py
@@ -24,7 +24,7 @@
 
 
 KX_ORDER = [
-    ((z + 7) % 8) * 8 + ((2 - x) % 4) * 2 + 1 - core
+    ((z + 6) % 8) * 8 + ((2 - x) % 4) * 2 + 1 - core
     for z in range(8)
     for x in range(4)
     for core in range(2)

time: 41.7 us -> 41.8 us (level)
  no operation moved by 1% of the time
where the time goes in v8:
time: 41.8 us; the launch traced here: 41.4 us
  blocking collectives  36.9 us (88%)
  Pallas kernels  3.81 us (9%)
  between operations  0.68 us (2%)
    all_to_all x2, blocking collectives, exchange(): lax.all_to_all(sent, axis, split_axis=0, concat_axis=0, tiled=True, axis_...  36.9 us
    pallas_call x1, Pallas kernels, on_device(): pl.pallas_call(x_kernel, out_shape=jax.ShapeDtypeStruct((KXW, 1, 2 * LINE...  1.93 us
    pallas_call x1, Pallas kernels, on_device(): pl.pallas_call(y_kernel, out_shape=(out, out), in_specs=[vmem] * 5, out_s...  1.35 us

profile of v8, /device:TPU:1, one launch (start us, length us, event | category | flops | bytes accessed | tf_op | source)
XLA Modules:
  0.0 41.4 jit_solution(13696046493731503920)
XLA Ops:
  0.6 1.9 %x_lines.1 = f32[64,1,576]{2,1,0:T(1,128)S(1)} custom-call(s32[1,144]{1,0:T(1,128)} %bitcast.3, s32[1,144]{1,0:T(1,128)} %bitcast.4, s32[1,144]{1,0:T(1,128)} %bitcast.5, f32[144,768]{1,0:T(8,128)} %values_hbm.1, bf16[384,256]{1,0:T(8,128)(2,1)} %constant.11.clone.table_hbm), custom_call_target="tpu_custom_call" | custom-call | tf_op jit(solution)/shard_map/x_lines/pallas_call | solution.py:293
  2.6 0.0 copy-start.3
  2.6 0.0 copy-start.4
  2.6 22.3 %all_to_all.10.in_ref = f32[64,1,576]{2,1,0:T(1,128)S(1)} all-to-all(f32[64,1,576]{2,1,0:T(1,128)S(1)} %x_lines.1), channel_id=1, replica_groups={{424,416,408,400,392,384,440,432,488,480,472,464,456,448,504,496,40,32,..., dimensions={0} | all-to-all | bytes 294912 | tf_op jit(solution)/shard_map/all_to_all | solution.py:278
  24.9 0.0 copy-done.3
  24.9 0.0 copy-done.4
  24.9 0.0 copy-start.2
  24.9 0.5 %z_rows.1 = f32[8,72,128]{2,1,0:T(8,128)S(1)} custom-call(f32[64,1,576]{2,1,0:T(1,128)S(1)} %all_to_all.10.in_ref, bf16[384,256]{1,0:T(8,128)(2,1)S(1)} %copy-done.3, f32[16,128]{1,0:T(8,128)S(1)} %copy-done.4), custom_call_target="tpu_custom_call" | custom-call | tf_op jit(solution)/shard_map/z_rows/pallas_call | solution.py:316
  25.4 0.0 copy-start
  25.4 0.0 copy-start.1
  25.4 14.6 %all_to_all.11.in_ref = f32[8,72,128]{2,1,0:T(8,128)S(1)} all-to-all(f32[8,72,128]{2,1,0:T(8,128)S(1)} %z_rows.1), channel_id=1, replica_groups={{5,6,7,0,1,2,3,4},{13,14,15,8,9,10,11,12},{21,22,23,16,17,18,19,20},{29..., dimensions={0} | all-to-all | bytes 589824 | tf_op jit(solution)/shard_map/all_to_all | solution.py:278
  40.0 0.0 copy-done.2
  40.0 0.0 copy-done
  40.0 0.0 copy-done.1
  40.0 1.3 %y_rows.1 = (f32[1,96,768]{2,1,0:T(8,128)}, f32[1,96,768]{2,1,0:T(8,128)}) custom-call(f32[8,72,128]{2,1,0:T(8,128)S(1)} %all_to_all.11.in_ref, f32[1,96,768]{2,1,0:T(8,128)S(1)} %copy-done, f32[1,96,768]{2,1,0:T(8,128)S(1)} %copy-done.1, bf16[384,256]{1,0:T(8,128)(2,1)S(1)} %copy-done.2, f32[16,128]{1,0:T(8,128)S(1)} %copy-done.4), custom_call_target="tpu_custom_call" | custom-call | tf_op jit(solution)/shard_map/y_rows/pallas_call | solution.py:324
Async XLA Ops:
  2.6 22.3 %copy-start.3 = (bf16[384,256]{1,0:T(8,128)(2,1)S(1)}, bf16[384,256]{1,0:T(8,128)(2,1)}, u32[]{:S(2)}) copy-start(bf16[384,256]{1,0:T(8,128)(2,1)} %constant.8.clone.table_ref) | copy-start | bytes 589828
  2.6 22.3 %copy-start.4 = (f32[16,128]{1,0:T(8,128)S(1)}, f32[16,128]{1,0:T(8,128)}, u32[]{:S(2)}) copy-start(f32[16,128]{1,0:T(8,128)} %constant.10.clone.twiddle_ref) | copy-start | bytes 24580
  24.9 15.2 %copy-start.2 = (bf16[384,256]{1,0:T(8,128)(2,1)S(1)}, bf16[384,256]{1,0:T(8,128)(2,1)}, u32[]{:S(2)}) copy-start(bf16[384,256]{1,0:T(8,128)(2,1)} %constant.9.clone.table_ref) | copy-start | bytes 589828
  25.4 14.6 %copy-start = (f32[1,96,768]{2,1,0:T(8,128)S(1)}, f32[1,96,768]{2,1,0:T(8,128)}, u32[]{:S(2)}) copy-start(f32[1,96,768]{2,1,0:T(8,128)} %real_ref.1) | copy-start | bytes 884740
  25.4 14.6 %copy-start.1 = (f32[1,96,768]{2,1,0:T(8,128)S(1)}, f32[1,96,768]{2,1,0:T(8,128)}, u32[]{:S(2)}) copy-start(f32[1,96,768]{2,1,0:T(8,128)} %imag_ref.1) | copy-start | bytes 884740
